TPU v7x, 32 devices: a whole 2x2x4 slice. The times are simulated.
32 devices in a mesh: temporal: 16 (over z, y, core), ulysses: 2 (over x).
Axes of the slice: x: 2, y: 2, z: 4, core: 2. Of those that a mesh axis runs over, the one named last changes fastest.
Arguments:
- queries: bfloat16 [16384, 1536], P(('temporal', 'ulysses')), may hold values from -12 to 12
- keys: bfloat16 [16384, 1536], P(('temporal', 'ulysses')), may hold values from -12 to 12
- values: bfloat16 [16384, 1536], P(('temporal', 'ulysses')), may hold values from -6 to 6
- tile_list: int32 [128, 5], P('temporal'), may hold values from 0 to 127, as said below
- counts: int32 [128], P('temporal'), may hold values from 1 to 5, as said below
- out_weight: bfloat16 [1536, 1536], replicated, may hold values from -0.15625 to 0.15625
Outputs:
- projected: bfloat16 [16384, 1536], P(('temporal', 'ulysses'))
Inputs may be any that keep to these rules, and one draw needn't show every extreme that they name: `tile_list`: every id in row g lies within 3 of g and in the same video as g; the first entry is g itself; the first counts[g] entries are distinct; entries past counts[g] equal g. `counts`: some tile has 5 live entries.
All inputs are finite; a program needn't handle non-finite values.
Results may differ from a plain program's by a relative error of at most 0.0056.
Values may be sent and summed in bfloat16 or wider, within the bound.
No kernel may reach another device: no remote copies, remote signals or barrier semaphores. Data moves between devices by JAX's collectives and lax.ppermute only.
A program may use at most 64 MiB of HBM per device.

v0:
```python
import functools
import math

import jax
import jax.numpy as jnp
from jax import lax
from jax.experimental import pallas as pl
from jax.experimental.pallas import tpu as pltpu
from jax.sharding import PartitionSpec as P

HD = 128
TILE = 128
REACH = 3
STRIP = 256
HBM = pl.BlockSpec(memory_space=pltpu.HBM)
VMEM = pl.BlockSpec(memory_space=pltpu.VMEM)
SMEM = pl.BlockSpec(memory_space=pltpu.SMEM)
VMEM_LIMIT = 14 * 1024 * 1024
VMEM_WHOLE = 63 * 1024 * 1024


def split_heads(heads):
    sizes = []
    for share in (3 / 12, 3 / 12, 3 / 12, 2 / 12):
        size = min(max(1, round(share * heads)), heads - sum(sizes) - 1)
        if size > 0:
            sizes.append(size)
    return sizes + [heads - sum(sizes)]


def cut_spots(tiles, rim):
    member = lax.axis_index("ulysses")
    return [member * (tiles - rim), (1 - member) * rim]


def piece_spots(tiles, hops, rim, relay, parted):
    if not relay:
        return [tiles * hops] + [tiles * i for i in range(2 * hops + 1) if i != hops]
    member = lax.axis_index("ulysses")
    if not parted:
        return [tiles, 2 * tiles * (1 - member), 2 * tiles * member]
    return [
        tiles,
        (1 - member) * (3 * tiles - rim),
        (1 - member) * 2 * tiles + member * rim,
        (1 - member) * (tiles - rim) + member * 2 * tiles,
    ]


def pack_kernel(groups, q_groups, cuts, *refs):
    refs = list(refs)
    q_ref, k_ref, v_ref = [refs.pop(0) for _ in range(3)]
    outs = [refs.pop(0) for _ in groups]
    q_outs = [refs.pop(0) for _ in q_groups]
    cut_outs = [refs.pop(0) for _ in cuts]
    k_buf, out_buf, q_buf, sems, q_sems, cut_sems = refs
    rows = k_ref.shape[0]
    jobs, q_jobs = [], []
    for out, (low, size) in zip(outs, groups):
        for h in range(size):
            at = len(jobs)
            cols = pl.ds((low + h) * HD, HD)
            jobs.append(
                (
                    pltpu.make_async_copy(k_ref.at[:, cols], k_buf.at[at], sems.at[at, 0]),
                    pltpu.make_async_copy(v_ref.at[:, cols], out_buf.at[at, 1], sems.at[at, 1]),
                    pltpu.make_async_copy(out_buf.at[at], out.at[h], sems.at[at, 2]),
                )
            )
    for out, (low, size) in zip(q_outs, q_groups):
        for h in range(size):
            at = len(q_jobs)
            cols = pl.ds((low + h) * HD, HD)
            q_jobs.append(
                (
                    pltpu.make_async_copy(q_ref.at[:, cols], q_buf.at[at], q_sems.at[at, 0]),
                    pltpu.make_async_copy(q_buf.at[at], out.at[h], q_sems.at[at, 1]),
                )
            )
    for load_k, load_v, _ in jobs:
        load_k.start()
        load_v.start()
    for load, _ in q_jobs:
        load.start()
    for at, (load_k, load_v, store) in enumerate(jobs):
        load_k.wait()
        for tile in range(rows // TILE):
            span = slice(tile * TILE, (tile + 1) * TILE)
            out_buf[at, 0, span] = k_buf[at, span].T
        load_v.wait()
        store.start()
    cut_jobs = []
    spots = cut_spots(rows // TILE, cuts[0][-1]) if cuts else []
    for (start, size, which, extent), out in zip(cuts, cut_outs):
        part = pl.ds(pl.multiple_of(spots[which] * TILE, TILE), extent * TILE)
        for h in range(size):
            source = out_buf.at[start - groups[0][0] + h, :, part]
            cut_jobs.append(pltpu.make_async_copy(source, out.at[h], cut_sems.at[len(cut_jobs)]))
            cut_jobs[-1].start()
    for load, store in q_jobs:
        load.wait()
        store.start()
    for _, _, store in jobs:
        store.wait()
    for _, store in q_jobs:
        store.wait()
    for store in cut_jobs:
        store.wait()


def pack(queries, keys, values, groups, q_groups, cuts, limit):
    rows = keys.shape[0]
    heads = sum(size for _, size in groups)
    q_heads = sum(size for _, size in q_groups)
    shapes = [(size, 2, rows, HD) for _, size in groups] + [(size, rows, HD) for _, size in q_groups]
    shapes += [(size, 2, extent * TILE, HD) for _, size, _, extent in cuts]
    return pl.pallas_call(
        functools.partial(pack_kernel, groups, q_groups, cuts),
        out_shape=[jax.ShapeDtypeStruct(shape, keys.dtype) for shape in shapes],
        in_specs=[HBM] * 3,
        out_specs=[HBM] * len(shapes),
        scratch_shapes=[
            pltpu.VMEM((heads, rows, HD), keys.dtype),
            pltpu.VMEM((heads, 2, rows, HD), keys.dtype),
            pltpu.VMEM((max(q_heads, 1), rows, HD), keys.dtype),
            pltpu.SemaphoreType.DMA((heads, 3)),
            pltpu.SemaphoreType.DMA((max(q_heads, 1), 2)),
            pltpu.SemaphoreType.DMA((max(sum(size for _, size, _, _ in cuts), 1),)),
        ],
        compiler_params=pltpu.CompilerParams(vmem_limit_bytes=limit),
        cost_estimate=pl.CostEstimate(flops=0, bytes_accessed=8 * rows * heads * HD, transcendentals=0),
    )(queries, keys, values)


def attend_kernel(cfg, tiles_ref, counts_ref, q_ref, *refs):
    low, size, shifts, (hops, rim, relay, parted), early, has_acc, final = cfg
    refs = list(refs)
    piece_refs = [refs.pop(0) for _ in shifts]
    early_refs = [refs.pop(0) for _ in early or ()]
    w_ref = None if early is None else refs.pop(0)
    acc_ref = refs.pop(0) if has_acc else None
    out_ref, kv_buf = refs[:2]
    rows = q_ref.shape[1]
    tiles = rows // TILE
    slots = tiles_ref.shape[1]
    spans = (2 * hops + 1) * rows
    spots = piece_spots(tiles, hops, rim, relay, parted)
    member, members = lax.axis_index("ulysses"), lax.axis_size("ulysses")
    first = (lax.axis_index("temporal") * members + member - hops) * tiles
    att_buf, lead = out_ref, 0
    if early is not None:
        att_buf = refs[2]
        for extent, ref in zip(early, early_refs):
            att_buf[:, lead * HD : (lead + extent) * HD] = ref[...]
            lead += extent

    scale = math.log2(math.e) / math.sqrt(HD)
    zeros = jnp.zeros((TILE, HD), jnp.bfloat16)
    places, v_places, ones = [], [], []
    for tile in range(tiles):
        row = member * tiles + tile
        live = counts_ref[row]
        at = [pl.multiple_of((tiles_ref[row, j] - first) * TILE, TILE) for j in range(slots)]
        places.append(at)
        v_places.append([pl.multiple_of(jnp.where(j < live, at[j], spans), TILE) for j in range(slots)])
        ones.append([zeros + jnp.where(j < live, 1.0, 0.0).astype(jnp.bfloat16) for j in range(slots)])

    def scores(h, tile):
        k = jnp.concatenate([kv_buf[h % 2, 0, pl.ds(p, TILE)] for p in places[tile]], axis=1)
        q = q_ref[h, tile * TILE : (tile + 1) * TILE]
        return jnp.dot(q, k, preferred_element_type=jnp.float32)

    def finish(h, tile, s):
        top = jnp.max(s, axis=1, keepdims=True)
        p = jnp.exp2((s - top) * scale).astype(jnp.bfloat16)
        v = jnp.concatenate(
            [
                jnp.concatenate([kv_buf[h % 2, 1, pl.ds(at, TILE)], one], axis=1)
                for at, one in zip(v_places[tile], ones[tile])
            ],
            axis=0,
        )
        mixed = jnp.dot(p, v, preferred_element_type=jnp.float32)
        here = slice(tile * TILE, (tile + 1) * TILE)
        att_buf[here, (lead + h) * HD : (lead + h + 1) * HD] = (mixed[:, :HD] / mixed[:, HD:]).astype(jnp.bfloat16)

    def ready(h):
        for i, ref in enumerate(piece_refs):
            place = pl.ds(pl.multiple_of(spots[i] * TILE, TILE), ref.shape[2])
            for part in range(2):
                kv_buf[h % 2, part, place] = ref[h + shifts[i], part]
        kv_buf[h % 2, 1, spans : spans + TILE] = zeros

    jobs = [(h, tile) for h in range(size) for tile in range(tiles)]
    ready(0)
    ahead = scores(*jobs[0])
    for i, (h, tile) in enumerate(jobs):
        now = ahead
        if i + 1 < len(jobs):
            if jobs[i + 1][0] != h:
                ready(h + 1)
            ahead = scores(*jobs[i + 1])
        finish(h, tile, now)

    if early is None:
        return
    stores = []
    out_buf, out_sems = refs[3:] if final else (out_ref, None)
    for i, at in enumerate(range(0, out_buf.shape[1], STRIP)):
        here = slice(at, min(at + STRIP, out_buf.shape[1]))
        weights = w_ref[(low - lead) * HD : (low + size) * HD, here]
        part = jnp.dot(att_buf[...], weights, preferred_element_type=jnp.float32)
        if has_acc:
            part = part + acc_ref[:, here]
        out_buf[:, here] = part.astype(out_buf.dtype)
        if final:
            cols = pl.ds(at, here.stop - at)
            stores.append(pltpu.make_async_copy(out_buf.at[:, cols], out_ref.at[:, cols], out_sems.at[i]))
            stores[-1].start()
    for copy in stores:
        copy.wait()


def attend(tile_list, counts, layout, queries, pieces, shifts, span, early, out_weight, acc, final):
    rows = queries.shape[1]
    low, size = span
    reach = (2 * layout[0] + 1) * rows
    width = out_weight.shape[1]
    bf16 = jnp.bfloat16
    operands = [tile_list, counts, queries, *pieces]
    scratch = [pltpu.VMEM((2, 2, reach + TILE, HD), bf16)]
    parts = None
    out_shape = jax.ShapeDtypeStruct((rows, size * HD), bf16)
    if early is not None:
        parts = tuple(part.shape[1] // HD for part in early)
        operands += [*early, out_weight]
        if acc is not None:
            operands.append(acc)
        scratch.append(pltpu.VMEM((rows, (size + sum(parts)) * HD), bf16))
        out_shape = jax.ShapeDtypeStruct((rows, width), bf16 if final else jnp.float32)
        if final:
            scratch += [pltpu.VMEM((rows, width), bf16), pltpu.SemaphoreType.DMA((-(-width // STRIP),))]
    return pl.pallas_call(
        functools.partial(
            attend_kernel, (low, size, shifts, layout, parts, acc is not None, final)
        ),
        out_shape=out_shape,
        in_specs=[SMEM] * 2 + [VMEM] * (len(operands) - 2),
        out_specs=HBM if final else VMEM,
        scratch_shapes=scratch,
        compiler_params=pltpu.CompilerParams(vmem_limit_bytes=VMEM_LIMIT),
        cost_estimate=pl.CostEstimate(flops=0, bytes_accessed=0, transcendentals=0),
    )(*operands)


def after(array, *others):
    return lax.optimization_barrier((array, *others))[0]


def on_device(queries, keys, values, tile_list, counts, out_weight):
    rows, model = queries.shape
    tiles = rows // TILE
    groups, members = lax.axis_size("temporal"), lax.axis_size("ulysses")
    total = groups * members
    both = ("temporal", "ulysses")
    hops = -(-REACH // tiles)
    relay = members == 2 and hops == 1
    rim = min(REACH, tiles)

    spans, low = [], 0
    for size in split_heads(model // HD):
        spans.append((low, size))
        low += size
    count = len(spans)
    sent = pack(queries, keys, values, spans[:1], [], [], VMEM_WHOLE)
    split = max(1, count - 2) if relay and tiles > rim else count
    cuts = [(low, size, 0, rim) for low, size in spans[split:]]
    if cuts:
        rest_low = spans[split][0]
        cuts.append((rest_low, model // HD - rest_low, 1, tiles - rim))
    laid = pack(queries, after(keys, *sent), values, spans, spans, cuts, VMEM_LIMIT)
    blocks, heads_of, parts = laid[:count], laid[count : 2 * count], laid[2 * count :]
    sent = [*sent, *blocks[1:split], *parts]

    onward = [(2 * g, 2 * g + 2) for g in range(groups - 1)]
    onward += [(2 * g + 3, 2 * g + 1) for g in range(groups - 1)]
    near = []
    for i, block in enumerate(sent):
        if relay:
            with jax.named_scope(f"partner_{i}" if i < count else f"rest_{i}"):
                near.append([lax.ppermute(block, "ulysses", [(0, 1), (1, 0)])])
        else:
            near.append(
                [
                    lax.ppermute(block, both, [(j, j - o) for j in range(total) if 0 <= j - o < total])
                    for o in range(-hops, hops + 1)
                    if o
                ]
            )

    ends = [j for j in (count - 4, count - 2) if j >= 0] + [count - 1]
    results, acc, begin = [], None, 0
    for i in range(count + 1):
        if i < count:
            pieces = [blocks[i], *near[i]]
            shifts = [0] * len(pieces)
            if i >= split:
                pieces += near[count]
                shifts.append(spans[i][0] - rest_low)
            if relay:
                back = 3 if i == count - 1 else 2
                gate = near[i][0] if i < back else after(near[i][0], results[i - back])
                with jax.named_scope(f"onward_{i}"):
                    pieces.append(lax.ppermute(gate, both, onward))
                shifts.append(0)
        if i >= 1:
            j = i - 1
            final = i == count
            early = results[begin:] if j in ends else None
            layout = (hops, rim, relay, j >= split)
            with jax.named_scope(f"attend_{j}"):
                result = attend(
                    tile_list, counts, layout, heads_of[j], *held, spans[j], early, out_weight,
                    None if early is None else acc, final,
                )
            results.append(result)
            if early is not None:
                acc, begin = result, i
        held = pieces, tuple(shifts)
    return results[-1]


def solution(mesh):
    return jax.shard_map(
        on_device,
        mesh=mesh,
        in_specs=(
            P(("temporal", "ulysses"), None),
            P(("temporal", "ulysses"), None),
            P(("temporal", "ulysses"), None),
            P("temporal", None),
            P("temporal"),
            P(),
        ),
        out_specs=P(("temporal", "ulysses"), None),
        check_vma=False,
    )
```

profile of v0, /device:TPU:8, one launch (start us, length us, event | category | flops | bytes accessed | tf_op | source)
XLA Modules:
  0.0 81.2 jit_solution(4735168703896434378)
XLA Ops:
  0.0 2.1 %shard_map.64 = bf16[3,2,512,128]{3,2,1,0:T(8,128)(2,1)} custom-call(bf16[512,1536]{1,0:T(8,128)(2,1)} %refs_0_.3, bf16[512,1536]{1,0:T(8,128)(2,1)} %refs_1_.2, bf16[512,1536]{1,0:T(8,128)(2,1)} %refs_2_.3), custom_call_target="tpu_custom_call" | custom-call | bytes 1572864 | tf_op jit(solution)/shard_map/pallas_call | solution.py:117
  2.1 1.6 %collective-permute-start.4 = (bf16[3,2,512,128]{3,2,1,0:T(8,128)(2,1)}, bf16[3,2,512,128]{3,2,1,0:T(8,128)(2,1)S(1)}, u32[]{:S(2)}, u32[]{:S(2)}) collective-permute-start(bf16[3,2,512,128]{3,2,1,0:T(8,128)(2,1)} %shard_map.64), channel_id=1, source_target_pairs={{0,1},{1,0},{2,3},{3,2},{4,5},{5,4},{6,7},{7,6},{8,9},{9,8},{10,11... | collective-permute-start | bytes 2359304 | tf_op jit(solution)/shard_map/partner_0/ppermute | solution.py:291
  3.7 1.4 %copy-done = bf16[512,1536]{1,0:T(8,128)(2,1)S(1)} copy-done((bf16[512,1536]{1,0:T(8,128)(2,1)S(1)}, bf16[512,1536]{1,0:T(8,128)(2,1)}, u32[]{:S(2)}) %copy-start) | copy-done | bytes 1572888
  5.1 1.4 %copy-done.1 = bf16[512,1536]{1,0:T(8,128)(2,1)S(1)} copy-done((bf16[512,1536]{1,0:T(8,128)(2,1)S(1)}, bf16[512,1536]{1,0:T(8,128)(2,1)}, u32[]{:S(2)}) %copy-start.1) | copy-done | bytes 1572888
  6.5 1.4 %copy-done.2 = bf16[512,1536]{1,0:T(8,128)(2,1)S(1)} copy-done((bf16[512,1536]{1,0:T(8,128)(2,1)S(1)}, bf16[512,1536]{1,0:T(8,128)(2,1)}, u32[]{:S(2)}) %copy-start.2) | copy-done | bytes 1572888
  7.9 5.3 %shard_map.65 = (bf16[3,2,512,128]{3,2,1,0:T(8,128)(2,1)S(1)}, bf16[3,2,512,128]{3,2,1,0:T(8,128)(2,1)S(1)}, bf16[3,2,512,128]{3,2,1,0:T(8,128)(2,1)S(1)}, bf16[...) custom-call(bf16[512,1536]{1,0:T(8,128)(2,1)S(1)} %copy-done, ...), custom_call_target="tpu_custom_call" | custom-call | bytes 6291456 | tf_op jit(solution)/shard_map/pallas_call | solution.py:117
  14.2 8.7 %collective-permute-done.4.refs_1_ = bf16[3,2,512,128]{3,2,1,0:T(8,128)(2,1)S(1)} collective-permute-done((bf16[3,2,512,128]{3,2,1,0:T(8,128)(2,1)}, bf16[3,2,512,128]{3,2,1,0:T(8,128)(2,1)S(1)}, u32[]{:S(2)}, u32[]{:S(2)}) %collective-permute-start.4) | collective-permute-done | bytes 786464 | tf_op jit(solution)/shard_map/partner_0/ppermute | solution.py:291
  22.9 1.9 %collective-permute-start.5 = (bf16[3,2,512,128]{3,2,1,0:T(8,128)(2,1)S(1)}, bf16[3,2,512,128]{3,2,1,0:T(8,128)(2,1)S(1)}, u32[]{:S(2)}, u32[]{:S(2)}) collective-permute-start(bf16[3,2,512,128]{3,2,1,0:T(8,128)(2,1)S(1)} %collective-permute-done.4.refs_1_), channel_id=1, source_target_pairs={{0,2},{2,4},{4,6},{6,8},{8,10},{10,12},{12,14},{14,16},{16,18},{18... | collective-permute-start | bytes 2359304 | tf_op jit(solution)/shard_map/onward_0/ppermute | solution.py:314
  24.8 1.6 %collective-permute-start.9 = (bf16[3,2,512,128]{3,2,1,0:T(8,128)(2,1)S(1)}, bf16[3,2,512,128]{3,2,1,0:T(8,128)(2,1)S(1)}, u32[]{:S(2)}, u32[]{:S(2)}) collective-permute-start(bf16[3,2,512,128]{3,2,1,0:T(8,128)(2,1)S(1)} %get-tuple-element.37.refs_0_), channel_id=1, source_target_pairs={{0,1},{1,0},{2,3},{3,2},{4,5},{5,4},{6,7},{7,6},{8,9},{9,8},{10,11... | collective-permute-start | bytes 2359304 | tf_op jit(solution)/shard_map/partner_2/ppermute | solution.py:291
  26.3 13.4 %collective-permute-done.2.refs_1_ = bf16[3,2,512,128]{3,2,1,0:T(8,128)(2,1)S(1)} collective-permute-done((bf16[3,2,512,128]{3,2,1,0:T(8,128)(2,1)S(1)}, bf16[3,2,512,128]{3,2,1,0:T(8,128)(2,1)S(1)}, u32[]{:S(2)}, u32[]{:S(2)}) %collective-permute-start.2) | collective-permute-done | bytes 786464 | tf_op jit(solution)/shard_map/partner_1/ppermute | solution.py:291
  39.7 1.9 %collective-permute-start.3 = (bf16[3,2,512,128]{3,2,1,0:T(8,128)(2,1)S(1)}, bf16[3,2,512,128]{3,2,1,0:T(8,128)(2,1)S(1)}, u32[]{:S(2)}, u32[]{:S(2)}) collective-permute-start(bf16[3,2,512,128]{3,2,1,0:T(8,128)(2,1)S(1)} %collective-permute-done.2.refs_1_), channel_id=1, source_target_pairs={{0,2},{2,4},{4,6},{6,8},{8,10},{10,12},{12,14},{14,16},{16,18},{18... | collective-permute-start | bytes 2359304 | tf_op jit(solution)/shard_map/onward_1/ppermute | solution.py:314
  41.6 1.6 %collective-permute-start.7 = (bf16[2,2,384,128]{3,2,1,0:T(8,128)(2,1)S(1)}, bf16[2,2,384,128]{3,2,1,0:T(8,128)(2,1)S(1)}, u32[]{:S(2)}, u32[]{:S(2)}) collective-permute-start(bf16[2,2,384,128]{3,2,1,0:T(8,128)(2,1)S(1)} %get-tuple-element.34), channel_id=1, source_target_pairs={{0,1},{1,0},{2,3},{3,2},{4,5},{5,4},{6,7},{7,6},{8,9},{9,8},{10,11... | collective-permute-start | bytes 1179656 | tf_op jit(solution)/shard_map/partner_3/ppermute | solution.py:291
  43.2 2.5 %attend_0.1.refs_3_ = bf16[512,384]{1,0:T(8,128)(2,1)S(1)} custom-call(s32[8,5]{1,0:T(8,128)S(1)} %copy-done.3, s32[8]{0:T(128)S(1)} %copy-done.4, bf16[3,512,128]{2,1,0:T(8,128)(2,1)S(1)} %get-tuple-element.29.q_ref, bf16[3,2,512,128]{3,2,1,0:T(8,128)(2,1)S(1)} %get-tuple-element.30.refs_0_, bf16[3,2,512,128]{3,2,1,0:T(8,128)(2,1)S(1)} %collective-permute-done.4.refs_1_, ...), custom_call_target="tpu_custom_call" | custom-call | tf_op jit(solution)/shard_map/attend_0/pallas_call | solution.py:243
  45.7 10.8 %collective-permute-done.9.refs_1_ = bf16[3,2,512,128]{3,2,1,0:T(8,128)(2,1)S(1)} collective-permute-done((bf16[3,2,512,128]{3,2,1,0:T(8,128)(2,1)S(1)}, bf16[3,2,512,128]{3,2,1,0:T(8,128)(2,1)S(1)}, u32[]{:S(2)}, u32[]{:S(2)}) %collective-permute-start.9) | collective-permute-done | bytes 786464 | tf_op jit(solution)/shard_map/partner_2/ppermute | solution.py:291
  56.6 1.9 %collective-permute-start.10 = (bf16[3,2,512,128]{3,2,1,0:T(8,128)(2,1)S(1)}, bf16[3,2,512,128]{3,2,1,0:T(8,128)(2,1)S(1)}, u32[]{:S(2)}, u32[]{:S(2)}) collective-permute-start(bf16[3,2,512,128]{3,2,1,0:T(8,128)(2,1)S(1)} %collective-permute-done.9.refs_1_), channel_id=1, source_target_pairs={{0,2},{2,4},{4,6},{6,8},{8,10},{10,12},{12,14},{14,16},{16,18},{18... | collective-permute-start | bytes 2359304 | tf_op jit(solution)/shard_map/onward_2/ppermute | solution.py:314
  58.5 1.6 %collective-permute-start = (bf16[1,2,384,128]{3,2,1,0:T(8,128)(2,1)S(1)}, bf16[1,2,384,128]{3,2,1,0:T(8,128)(2,1)S(1)}, u32[]{:S(2)}, u32[]{:S(2)}) collective-permute-start(bf16[1,2,384,128]{3,2,1,0:T(8,128)(2,1)S(1)} %get-tuple-element.25), channel_id=1, source_target_pairs={{0,1},{1,0},{2,3},{3,2},{4,5},{5,4},{6,7},{7,6},{8,9},{9,8},{10,11... | collective-permute-start | bytes 589832 | tf_op jit(solution)/shard_map/partner_4/ppermute | solution.py:291
  60.1 3.8 %attend_1.1.refs_6_ = f32[512,1536]{1,0:T(8,128)S(1)} custom-call(s32[8,5]{1,0:T(8,128)S(1)} %copy-done.3, s32[8]{0:T(128)S(1)} %copy-done.4, bf16[3,512,128]{2,1,0:T(8,128)(2,1)S(1)} %get-tuple-element.27.q_ref, bf16[3,2,512,128]{3,2,1,0:T(8,128)(2,1)S(1)} %get-tuple-element.28.refs_0_, bf16[3,2,512,128]{3,2,1,0:T(8,128)(2,1)S(1)} %collective-permute-done.2.refs_1_, ...), custom_call_target="tpu_custom_call" | custom-call | tf_op jit(solution)/shard_map/attend_1/pallas_call | solution.py:243
  63.9 1.0 %collective-permute-done.7.refs_1_ = bf16[2,2,384,128]{3,2,1,0:T(8,128)(2,1)S(1)} collective-permute-done((bf16[2,2,384,128]{3,2,1,0:T(8,128)(2,1)S(1)}, bf16[2,2,384,128]{3,2,1,0:T(8,128)(2,1)S(1)}, u32[]{:S(2)}, u32[]{:S(2)}) %collective-permute-start.7) | collective-permute-done | bytes 393248 | tf_op jit(solution)/shard_map/partner_3/ppermute | solution.py:291
  64.9 1.9 %collective-permute-start.8 = (bf16[2,2,384,128]{3,2,1,0:T(8,128)(2,1)S(1)}, bf16[2,2,384,128]{3,2,1,0:T(8,128)(2,1)S(1)}, u32[]{:S(2)}, u32[]{:S(2)}) collective-permute-start(bf16[2,2,384,128]{3,2,1,0:T(8,128)(2,1)S(1)} %collective-permute-done.7.refs_1_), channel_id=1, source_target_pairs={{0,2},{2,4},{4,6},{6,8},{8,10},{10,12},{12,14},{14,16},{16,18},{18... | collective-permute-start | bytes 1179656 | tf_op jit(solution)/shard_map/onward_3/ppermute | solution.py:314
  66.8 2.0 %collective-permute-start.1 = (bf16[3,2,128,128]{3,2,1,0:T(8,128)(2,1)S(1)}, bf16[3,2,128,128]{3,2,1,0:T(8,128)(2,1)S(1)}, u32[]{:S(2)}, u32[]{:S(2)}) collective-permute-start(bf16[3,2,128,128]{3,2,1,0:T(8,128)(2,1)S(1)} %get-tuple-element.26), channel_id=1, source_target_pairs={{0,1},{1,0},{2,3},{3,2},{4,5},{5,4},{6,7},{7,6},{8,9},{9,8},{10,11... | collective-permute-start | bytes 589832 | tf_op jit(solution)/shard_map/rest_5/ppermute | solution.py:291
  68.8 2.1 %collective-permute-start.6 = (bf16[1,2,384,128]{3,2,1,0:T(8,128)(2,1)S(1)}, bf16[1,2,384,128]{3,2,1,0:T(8,128)(2,1)S(1)}, u32[]{:S(2)}, u32[]{:S(2)}) collective-permute-start(bf16[1,2,384,128]{3,2,1,0:T(8,128)(2,1)S(1)} %collective-permute-done.refs_1_), channel_id=1, source_target_pairs={{0,2},{2,4},{4,6},{6,8},{8,10},{10,12},{12,14},{14,16},{16,18},{18... | collective-permute-start | bytes 589832 | tf_op jit(solution)/shard_map/onward_4/ppermute | solution.py:314
  70.9 2.6 %attend_2.1.refs_4_ = bf16[512,384]{1,0:T(8,128)(2,1)S(1)} custom-call(s32[8,5]{1,0:T(8,128)S(1)} %copy-done.3, s32[8]{0:T(128)S(1)} %copy-done.4, bf16[3,512,128]{2,1,0:T(8,128)(2,1)S(1)} %get-tuple-element.36.q_ref, bf16[3,2,512,128]{3,2,1,0:T(8,128)(2,1)S(1)} %get-tuple-element.37.refs_0_, bf16[3,2,512,128]{3,2,1,0:T(8,128)(2,1)S(1)} %collective-permute-done.9.refs_1_, ...), custom_call_target="tpu_custom_call" | custom-call | tf_op jit(solution)/shard_map/attend_2/pallas_call | solution.py:243
  75.0 3.2 %attend_3.1.refs_5_ = f32[512,1536]{1,0:T(8,128)S(1)} custom-call(s32[8,5]{1,0:T(8,128)S(1)} %copy-done.3, s32[8]{0:T(128)S(1)} %copy-done.4, bf16[2,512,128]{2,1,0:T(8,128)(2,1)S(1)} %get-tuple-element.32.q_ref, bf16[2,2,512,128]{3,2,1,0:T(8,128)(2,1)S(1)} %get-tuple-element.33.refs_0_, bf16[2,2,384,128]{3,2,1,0:T(8,128)(2,1)S(1)} %collective-permute-done.7.refs_1_, ...), custom_call_target="tpu_custom_call" | custom-call | tf_op jit(solution)/shard_map/attend_3/pallas_call | solution.py:243
  78.2 2.8 %attend_4.1 = bf16[512,1536]{1,0:T(8,128)(2,1)} custom-call(s32[8,5]{1,0:T(8,128)S(1)} %copy-done.3, s32[8]{0:T(128)S(1)} %copy-done.4, bf16[1,512,128]{2,1,0:T(8,128)(2,1)S(1)} %get-tuple-element.23.q_ref, bf16[1,2,512,128]{3,2,1,0:T(8,128)(2,1)S(1)} %get-tuple-element.24.refs_0_, bf16[1,2,384,128]{3,2,1,0:T(8,128)(2,1)S(1)} %collective-permute-done.refs_1_, ...), custom_call_target="tpu_custom_call" | custom-call | tf_op jit(solution)/shard_map/attend_4/pallas_call | solution.py:243
  (20 shorter events, 2.5 us)
Async XLA Ops:
  0.0 60.0 %slice-start = ((s8[4718592]{0:T(1024)(128)(4,1)}), s8[524288]{0:T(1024)(128)(4,1)S(1)}, s32[]{:S(2)}) async-start(s8[4718592]{0:T(1024)(128)(4,1)} %bitcast), calls=%async_computation | async-start | bytes 1048576
  2.1 57.9 %slice-start.1 = ((s8[4718592]{0:T(1024)(128)(4,1)}), s8[4194304]{0:T(1024)(128)(4,1)S(1)}, s32[]{:S(2)}) async-start(s8[4718592]{0:T(1024)(128)(4,1)} %bitcast), calls=%async_computation.1 | async-start | bytes 8388608
  2.1 20.7 %collective-permute-start.4 = (bf16[3,2,512,128]{3,2,1,0:T(8,128)(2,1)}, bf16[3,2,512,128]{3,2,1,0:T(8,128)(2,1)S(1)}, u32[]{:S(2)}, u32[]{:S(2)}) collective-permute-start(bf16[3,2,512,128]{3,2,1,0:T(8,128)(2,1)} %shard_map.64), channel_id=1, source_target_pairs={{0,1},{1,0},{2,3},{3,2},{4,5},{5,4},{6,7},{7,6},{8,9},{9,8},{10,11... | collective-permute-start | bytes 2359304 | tf_op jit(solution)/shard_map/partner_0/ppermute | solution.py:291
  3.7 1.4 %copy-start = (bf16[512,1536]{1,0:T(8,128)(2,1)S(1)}, bf16[512,1536]{1,0:T(8,128)(2,1)}, u32[]{:S(2)}) copy-start(bf16[512,1536]{1,0:T(8,128)(2,1)} %refs_0_.3) | copy-start | bytes 4718596
  5.1 1.4 %copy-start.1 = (bf16[512,1536]{1,0:T(8,128)(2,1)S(1)}, bf16[512,1536]{1,0:T(8,128)(2,1)}, u32[]{:S(2)}) copy-start(bf16[512,1536]{1,0:T(8,128)(2,1)} %refs_1_.2) | copy-start | bytes 4718596
  6.5 1.4 %copy-start.2 = (bf16[512,1536]{1,0:T(8,128)(2,1)S(1)}, bf16[512,1536]{1,0:T(8,128)(2,1)}, u32[]{:S(2)}) copy-start(bf16[512,1536]{1,0:T(8,128)(2,1)} %refs_2_.3) | copy-start | bytes 4718596
  7.9 35.3 %copy-start.3 = (s32[8,5]{1,0:T(8,128)S(1)}, s32[8,5]{1,0:T(8,128)}, u32[]{:S(2)}) copy-start(s32[8,5]{1,0:T(8,128)} %tiles_ref.9) | copy-start | bytes 484
  7.9 35.3 %copy-start.4 = (s32[8]{0:T(128)S(1)}, s32[8]{0:T(128)}, u32[]{:S(2)}) copy-start(s32[8]{0:T(128)} %counts_ref.9) | copy-start | bytes 100
  13.3 26.4 %collective-permute-start.2 = (bf16[3,2,512,128]{3,2,1,0:T(8,128)(2,1)S(1)}, bf16[3,2,512,128]{3,2,1,0:T(8,128)(2,1)S(1)}, u32[]{:S(2)}, u32[]{:S(2)}) collective-permute-start(bf16[3,2,512,128]{3,2,1,0:T(8,128)(2,1)S(1)} %get-tuple-element.28.refs_0_), channel_id=1, source_target_pairs={{0,1},{1,0},{2,3},{3,2},{4,5},{5,4},{6,7},{7,6},{8,9},{9,8},{10,11... | collective-permute-start | bytes 2359304 | tf_op jit(solution)/shard_map/partner_1/ppermute | solution.py:291
  22.9 20.3 %collective-permute-start.5 = (bf16[3,2,512,128]{3,2,1,0:T(8,128)(2,1)S(1)}, bf16[3,2,512,128]{3,2,1,0:T(8,128)(2,1)S(1)}, u32[]{:S(2)}, u32[]{:S(2)}) collective-permute-start(bf16[3,2,512,128]{3,2,1,0:T(8,128)(2,1)S(1)} %collective-permute-done.4.refs_1_), channel_id=1, source_target_pairs={{0,2},{2,4},{4,6},{6,8},{8,10},{10,12},{12,14},{14,16},{16,18},{18... | collective-permute-start | bytes 2359304 | tf_op jit(solution)/shard_map/onward_0/ppermute | solution.py:314
  24.8 31.8 %collective-permute-start.9 = (bf16[3,2,512,128]{3,2,1,0:T(8,128)(2,1)S(1)}, bf16[3,2,512,128]{3,2,1,0:T(8,128)(2,1)S(1)}, u32[]{:S(2)}, u32[]{:S(2)}) collective-permute-start(bf16[3,2,512,128]{3,2,1,0:T(8,128)(2,1)S(1)} %get-tuple-element.37.refs_0_), channel_id=1, source_target_pairs={{0,1},{1,0},{2,3},{3,2},{4,5},{5,4},{6,7},{7,6},{8,9},{9,8},{10,11... | collective-permute-start | bytes 2359304 | tf_op jit(solution)/shard_map/partner_2/ppermute | solution.py:291
  39.7 20.3 %collective-permute-start.3 = (bf16[3,2,512,128]{3,2,1,0:T(8,128)(2,1)S(1)}, bf16[3,2,512,128]{3,2,1,0:T(8,128)(2,1)S(1)}, u32[]{:S(2)}, u32[]{:S(2)}) collective-permute-start(bf16[3,2,512,128]{3,2,1,0:T(8,128)(2,1)S(1)} %collective-permute-done.2.refs_1_), channel_id=1, source_target_pairs={{0,2},{2,4},{4,6},{6,8},{8,10},{10,12},{12,14},{14,16},{16,18},{18... | collective-permute-start | bytes 2359304 | tf_op jit(solution)/shard_map/onward_1/ppermute | solution.py:314
  41.6 23.2 %collective-permute-start.7 = (bf16[2,2,384,128]{3,2,1,0:T(8,128)(2,1)S(1)}, bf16[2,2,384,128]{3,2,1,0:T(8,128)(2,1)S(1)}, u32[]{:S(2)}, u32[]{:S(2)}) collective-permute-start(bf16[2,2,384,128]{3,2,1,0:T(8,128)(2,1)S(1)} %get-tuple-element.34), channel_id=1, source_target_pairs={{0,1},{1,0},{2,3},{3,2},{4,5},{5,4},{6,7},{7,6},{8,9},{9,8},{10,11... | collective-permute-start | bytes 1179656 | tf_op jit(solution)/shard_map/partner_3/ppermute | solution.py:291
  56.6 14.3 %collective-permute-start.10 = (bf16[3,2,512,128]{3,2,1,0:T(8,128)(2,1)S(1)}, bf16[3,2,512,128]{3,2,1,0:T(8,128)(2,1)S(1)}, u32[]{:S(2)}, u32[]{:S(2)}) collective-permute-start(bf16[3,2,512,128]{3,2,1,0:T(8,128)(2,1)S(1)} %collective-permute-done.9.refs_1_), channel_id=1, source_target_pairs={{0,2},{2,4},{4,6},{6,8},{8,10},{10,12},{12,14},{14,16},{16,18},{18... | collective-permute-start | bytes 2359304 | tf_op jit(solution)/shard_map/onward_2/ppermute | solution.py:314
  58.5 10.3 %collective-permute-start = (bf16[1,2,384,128]{3,2,1,0:T(8,128)(2,1)S(1)}, bf16[1,2,384,128]{3,2,1,0:T(8,128)(2,1)S(1)}, u32[]{:S(2)}, u32[]{:S(2)}) collective-permute-start(bf16[1,2,384,128]{3,2,1,0:T(8,128)(2,1)S(1)} %get-tuple-element.25), channel_id=1, source_target_pairs={{0,1},{1,0},{2,3},{3,2},{4,5},{5,4},{6,7},{7,6},{8,9},{9,8},{10,11... | collective-permute-start | bytes 589832 | tf_op jit(solution)/shard_map/partner_4/ppermute | solution.py:291
  64.9 10.1 %collective-permute-start.8 = (bf16[2,2,384,128]{3,2,1,0:T(8,128)(2,1)S(1)}, bf16[2,2,384,128]{3,2,1,0:T(8,128)(2,1)S(1)}, u32[]{:S(2)}, u32[]{:S(2)}) collective-permute-start(bf16[2,2,384,128]{3,2,1,0:T(8,128)(2,1)S(1)} %collective-permute-done.7.refs_1_), channel_id=1, source_target_pairs={{0,2},{2,4},{4,6},{6,8},{8,10},{10,12},{12,14},{14,16},{16,18},{18... | collective-permute-start | bytes 1179656 | tf_op jit(solution)/shard_map/onward_3/ppermute | solution.py:314
  66.8 7.2 %collective-permute-start.1 = (bf16[3,2,128,128]{3,2,1,0:T(8,128)(2,1)S(1)}, bf16[3,2,128,128]{3,2,1,0:T(8,128)(2,1)S(1)}, u32[]{:S(2)}, u32[]{:S(2)}) collective-permute-start(bf16[3,2,128,128]{3,2,1,0:T(8,128)(2,1)S(1)} %get-tuple-element.26), channel_id=1, source_target_pairs={{0,1},{1,0},{2,3},{3,2},{4,5},{5,4},{6,7},{7,6},{8,9},{9,8},{10,11... | collective-permute-start | bytes 589832 | tf_op jit(solution)/shard_map/rest_5/ppermute | solution.py:291
  68.8 9.5 %collective-permute-start.6 = (bf16[1,2,384,128]{3,2,1,0:T(8,128)(2,1)S(1)}, bf16[1,2,384,128]{3,2,1,0:T(8,128)(2,1)S(1)}, u32[]{:S(2)}, u32[]{:S(2)}) collective-permute-start(bf16[1,2,384,128]{3,2,1,0:T(8,128)(2,1)S(1)} %collective-permute-done.refs_1_), channel_id=1, source_target_pairs={{0,2},{2,4},{4,6},{6,8},{8,10},{10,12},{12,14},{14,16},{16,18},{18... | collective-permute-start | bytes 589832 | tf_op jit(solution)/shard_map/onward_4/ppermute | solution.py:314
where the time goes:
time: 82.3 us; the launch traced here: 81.2 us
  waiting for transfers between devices  35.4 us (43%)
  Pallas kernels  22.4 us (27%)
  starting transfers between devices  18.8 us (23%)
  local copies, waits for them, and re-layouts  4.24 us (5%)
    ppermute x6, waiting for transfers between devices, on_device(): near.append([lax.ppermute(block, 'ulysses', [(0, 1), (1, 0)])])  34.5 us
    pallas_call x5, Pallas kernels, attend(): pl.pallas_call(functools.partial(attend_kernel, (low, size, shifts, layou...  14.9 us
    ppermute x5, starting transfers between devices, on_device(): pieces.append(lax.ppermute(gate, both, onward))  9.73 us
    ppermute x6, starting transfers between devices, on_device(): near.append([lax.ppermute(block, 'ulysses', [(0, 1), (1, 0)])])  9.1 us
    pallas_call x2, Pallas kernels, pack(): pl.pallas_call(functools.partial(pack_kernel, groups, q_groups, cuts), ou...  7.45 us
    unnamed x14, local copies, waits for them, and re-layouts  4.24 us
  transfers between devices with their start and end apart: 11, of which 6 were waited for; matrix products, arithmetic and copies ran while one was open for 0% of the time, Pallas kernels for 22%

commit v1 on v0

--- a/solution.py
+++ b/solution.py
@@ -133,11 +133,11 @@
 
 
 def attend_kernel(cfg, tiles_ref, counts_ref, q_ref, *refs):
-    low, size, shifts, (hops, rim, relay, parted), early, has_acc, final = cfg
+    low, size, shifts, (hops, rim, relay, parted), early, projects, has_acc, final = cfg
     refs = list(refs)
     piece_refs = [refs.pop(0) for _ in shifts]
     early_refs = [refs.pop(0) for _ in early or ()]
-    w_ref = None if early is None else refs.pop(0)
+    w_ref = refs.pop(0) if projects else None
     acc_ref = refs.pop(0) if has_acc else None
     out_ref, kv_buf = refs[:2]
     rows = q_ref.shape[1]
@@ -149,7 +149,7 @@
     first = (lax.axis_index("temporal") * members + member - hops) * tiles
     att_buf, lead = out_ref, 0
     if early is not None:
-        att_buf = refs[2]
+        att_buf = refs[2] if projects else out_ref
         for extent, ref in zip(early, early_refs):
             att_buf[:, lead * HD : (lead + extent) * HD] = ref[...]
             lead += extent
@@ -202,7 +202,7 @@
             ahead = scores(*jobs[i + 1])
         finish(h, tile, now)
 
-    if early is None:
+    if not projects:
         return
     stores = []
     out_buf, out_sems = refs[3:] if final else (out_ref, None)
@@ -225,7 +225,7 @@
     rows = queries.shape[1]
     low, size = span
     reach = (2 * layout[0] + 1) * rows
-    width = out_weight.shape[1]
+    projects = out_weight is not None
     bf16 = jnp.bfloat16
     operands = [tile_list, counts, queries, *pieces]
     scratch = [pltpu.VMEM((2, 2, reach + TILE, HD), bf16)]
@@ -233,16 +233,20 @@
     out_shape = jax.ShapeDtypeStruct((rows, size * HD), bf16)
     if early is not None:
         parts = tuple(part.shape[1] // HD for part in early)
-        operands += [*early, out_weight]
+        operands += early
+        out_shape = jax.ShapeDtypeStruct((rows, (size + sum(parts)) * HD), bf16)
+    if projects:
+        width = out_weight.shape[1]
+        operands.append(out_weight)
         if acc is not None:
             operands.append(acc)
-        scratch.append(pltpu.VMEM((rows, (size + sum(parts)) * HD), bf16))
+        scratch.append(pltpu.VMEM(out_shape.shape, bf16))
         out_shape = jax.ShapeDtypeStruct((rows, width), bf16 if final else jnp.float32)
         if final:
             scratch += [pltpu.VMEM((rows, width), bf16), pltpu.SemaphoreType.DMA((-(-width // STRIP),))]
     return pl.pallas_call(
         functools.partial(
-            attend_kernel, (low, size, shifts, layout, parts, acc is not None, final)
+            attend_kernel, (low, size, shifts, layout, parts, projects, acc is not None, final)
         ),
         out_shape=out_shape,
         in_specs=[SMEM] * 2 + [VMEM] * (len(operands) - 2),
@@ -298,7 +302,7 @@
                 ]
             )
 
-    ends = [j for j in (count - 4, count - 2) if j >= 0] + [count - 1]
+    ends = [j for j in (count - 4,) if j >= 0] + [count - 1]
     results, acc, begin = [], None, 0
     for i in range(count + 1):
         if i < count:
@@ -316,16 +320,19 @@
         if i >= 1:
             j = i - 1
             final = i == count
-            early = results[begin:] if j in ends else None
+            projects = j in ends
+            early = results[begin:] if projects or j == count - 2 else None
             layout = (hops, rim, relay, j >= split)
             with jax.named_scope(f"attend_{j}"):
                 result = attend(
-                    tile_list, counts, layout, heads_of[j], *held, spans[j], early, out_weight,
-                    None if early is None else acc, final,
+                    tile_list, counts, layout, heads_of[j], *held, spans[j], early,
+                    out_weight if projects else None, acc if projects else None, final,
                 )
             results.append(result)
-            if early is not None:
+            if projects:
                 acc, begin = result, i
+            elif early is not None:
+                begin = j
         held = pieces, tuple(shifts)
     return results[-1]
 

time: 82.3 us -> 81.8 us (level)
  transfers between devices with their start and end apart: 11 -> 11, of which waited for: 6 -> 7; matrix products, arithmetic and copies ran while one was open for 0% -> 0% of each run, Pallas kernels for 22% -> 20%
where the time goes in v1:
time: 81.8 us; the launch traced here: 80.8 us
  waiting for transfers between devices  35.5 us (43%)
  Pallas kernels  21.9 us (27%)
  starting transfers between devices  18.8 us (23%)
  local copies, waits for them, and re-layouts  4.24 us (5%)
    ppermute x6, waiting for transfers between devices, on_device(): near.append([lax.ppermute(block, 'ulysses', [(0, 1), (1, 0)])])  34.5 us
    pallas_call x5, Pallas kernels, attend(): pl.pallas_call(functools.partial(attend_kernel, (low, size, shifts, layou...  14.5 us
    ppermute x5, starting transfers between devices, on_device(): pieces.append(lax.ppermute(gate, both, onward))  9.73 us
    ppermute x6, starting transfers between devices, on_device(): near.append([lax.ppermute(block, 'ulysses', [(0, 1), (1, 0)])])  9.1 us
    pallas_call x2, Pallas kernels, pack(): pl.pallas_call(functools.partial(pack_kernel, groups, q_groups, cuts), ou...  7.45 us
    unnamed x14, local copies, waits for them, and re-layouts  4.24 us
  transfers between devices with their start and end apart: 11, of which 7 were waited for; matrix products, arithmetic and copies ran while one was open for 0% of the time, Pallas kernels for 20%

profile of v1, /device:TPU:8, one launch (start us, length us, event | category | flops | bytes accessed | tf_op | source)
XLA Modules:
  0.0 80.8 jit_solution(12971524685390636486)
XLA Ops:
  0.0 2.1 %shard_map.64 = bf16[3,2,512,128]{3,2,1,0:T(8,128)(2,1)} custom-call(bf16[512,1536]{1,0:T(8,128)(2,1)} %refs_0_.3, bf16[512,1536]{1,0:T(8,128)(2,1)} %refs_1_.2, bf16[512,1536]{1,0:T(8,128)(2,1)} %refs_2_.3), custom_call_target="tpu_custom_call" | custom-call | bytes 1572864 | tf_op jit(solution)/shard_map/pallas_call | solution.py:117
  2.1 1.6 %collective-permute-start.4 = (bf16[3,2,512,128]{3,2,1,0:T(8,128)(2,1)}, bf16[3,2,512,128]{3,2,1,0:T(8,128)(2,1)S(1)}, u32[]{:S(2)}, u32[]{:S(2)}) collective-permute-start(bf16[3,2,512,128]{3,2,1,0:T(8,128)(2,1)} %shard_map.64), channel_id=1, source_target_pairs={{0,1},{1,0},{2,3},{3,2},{4,5},{5,4},{6,7},{7,6},{8,9},{9,8},{10,11... | collective-permute-start | bytes 2359304 | tf_op jit(solution)/shard_map/partner_0/ppermute | solution.py:295
  3.7 1.4 %copy-done = bf16[512,1536]{1,0:T(8,128)(2,1)S(1)} copy-done((bf16[512,1536]{1,0:T(8,128)(2,1)S(1)}, bf16[512,1536]{1,0:T(8,128)(2,1)}, u32[]{:S(2)}) %copy-start) | copy-done | bytes 1572888
  5.1 1.4 %copy-done.1 = bf16[512,1536]{1,0:T(8,128)(2,1)S(1)} copy-done((bf16[512,1536]{1,0:T(8,128)(2,1)S(1)}, bf16[512,1536]{1,0:T(8,128)(2,1)}, u32[]{:S(2)}) %copy-start.1) | copy-done | bytes 1572888
  6.5 1.4 %copy-done.2 = bf16[512,1536]{1,0:T(8,128)(2,1)S(1)} copy-done((bf16[512,1536]{1,0:T(8,128)(2,1)S(1)}, bf16[512,1536]{1,0:T(8,128)(2,1)}, u32[]{:S(2)}) %copy-start.2) | copy-done | bytes 1572888
  7.9 5.3 %shard_map.65 = (bf16[3,2,512,128]{3,2,1,0:T(8,128)(2,1)S(1)}, bf16[3,2,512,128]{3,2,1,0:T(8,128)(2,1)S(1)}, bf16[3,2,512,128]{3,2,1,0:T(8,128)(2,1)S(1)}, bf16[...) custom-call(bf16[512,1536]{1,0:T(8,128)(2,1)S(1)} %copy-done, ...), custom_call_target="tpu_custom_call" | custom-call | bytes 6291456 | tf_op jit(solution)/shard_map/pallas_call | solution.py:117
  14.2 8.7 %collective-permute-done.4.refs_1_ = bf16[3,2,512,128]{3,2,1,0:T(8,128)(2,1)S(1)} collective-permute-done((bf16[3,2,512,128]{3,2,1,0:T(8,128)(2,1)}, bf16[3,2,512,128]{3,2,1,0:T(8,128)(2,1)S(1)}, u32[]{:S(2)}, u32[]{:S(2)}) %collective-permute-start.4) | collective-permute-done | bytes 786464 | tf_op jit(solution)/shard_map/partner_0/ppermute | solution.py:295
  22.9 1.9 %collective-permute-start.5 = (bf16[3,2,512,128]{3,2,1,0:T(8,128)(2,1)S(1)}, bf16[3,2,512,128]{3,2,1,0:T(8,128)(2,1)S(1)}, u32[]{:S(2)}, u32[]{:S(2)}) collective-permute-start(bf16[3,2,512,128]{3,2,1,0:T(8,128)(2,1)S(1)} %collective-permute-done.4.refs_1_), channel_id=1, source_target_pairs={{0,2},{2,4},{4,6},{6,8},{8,10},{10,12},{12,14},{14,16},{16,18},{18... | collective-permute-start | bytes 2359304 | tf_op jit(solution)/shard_map/onward_0/ppermute | solution.py:318
  24.8 1.6 %collective-permute-start.9 = (bf16[3,2,512,128]{3,2,1,0:T(8,128)(2,1)S(1)}, bf16[3,2,512,128]{3,2,1,0:T(8,128)(2,1)S(1)}, u32[]{:S(2)}, u32[]{:S(2)}) collective-permute-start(bf16[3,2,512,128]{3,2,1,0:T(8,128)(2,1)S(1)} %get-tuple-element.37.refs_0_), channel_id=1, source_target_pairs={{0,1},{1,0},{2,3},{3,2},{4,5},{5,4},{6,7},{7,6},{8,9},{9,8},{10,11... | collective-permute-start | bytes 2359304 | tf_op jit(solution)/shard_map/partner_2/ppermute | solution.py:295
  26.3 13.4 %collective-permute-done.2.refs_1_ = bf16[3,2,512,128]{3,2,1,0:T(8,128)(2,1)S(1)} collective-permute-done((bf16[3,2,512,128]{3,2,1,0:T(8,128)(2,1)S(1)}, bf16[3,2,512,128]{3,2,1,0:T(8,128)(2,1)S(1)}, u32[]{:S(2)}, u32[]{:S(2)}) %collective-permute-start.2) | collective-permute-done | bytes 786464 | tf_op jit(solution)/shard_map/partner_1/ppermute | solution.py:295
  39.7 1.9 %collective-permute-start.3 = (bf16[3,2,512,128]{3,2,1,0:T(8,128)(2,1)S(1)}, bf16[3,2,512,128]{3,2,1,0:T(8,128)(2,1)S(1)}, u32[]{:S(2)}, u32[]{:S(2)}) collective-permute-start(bf16[3,2,512,128]{3,2,1,0:T(8,128)(2,1)S(1)} %collective-permute-done.2.refs_1_), channel_id=1, source_target_pairs={{0,2},{2,4},{4,6},{6,8},{8,10},{10,12},{12,14},{14,16},{16,18},{18... | collective-permute-start | bytes 2359304 | tf_op jit(solution)/shard_map/onward_1/ppermute | solution.py:318
  41.6 1.6 %collective-permute-start.7 = (bf16[2,2,384,128]{3,2,1,0:T(8,128)(2,1)S(1)}, bf16[2,2,384,128]{3,2,1,0:T(8,128)(2,1)S(1)}, u32[]{:S(2)}, u32[]{:S(2)}) collective-permute-start(bf16[2,2,384,128]{3,2,1,0:T(8,128)(2,1)S(1)} %get-tuple-element.34), channel_id=1, source_target_pairs={{0,1},{1,0},{2,3},{3,2},{4,5},{5,4},{6,7},{7,6},{8,9},{9,8},{10,11... | collective-permute-start | bytes 1179656 | tf_op jit(solution)/shard_map/partner_3/ppermute | solution.py:295
  43.2 2.5 %attend_0.1.refs_3_ = bf16[512,384]{1,0:T(8,128)(2,1)S(1)} custom-call(s32[8,5]{1,0:T(8,128)S(1)} %copy-done.3, s32[8]{0:T(128)S(1)} %copy-done.4, bf16[3,512,128]{2,1,0:T(8,128)(2,1)S(1)} %get-tuple-element.29.q_ref, bf16[3,2,512,128]{3,2,1,0:T(8,128)(2,1)S(1)} %get-tuple-element.30.refs_0_, bf16[3,2,512,128]{3,2,1,0:T(8,128)(2,1)S(1)} %collective-permute-done.4.refs_1_, ...), custom_call_target="tpu_custom_call" | custom-call | tf_op jit(solution)/shard_map/attend_0/pallas_call | solution.py:247
  45.7 10.8 %collective-permute-done.9.refs_1_ = bf16[3,2,512,128]{3,2,1,0:T(8,128)(2,1)S(1)} collective-permute-done((bf16[3,2,512,128]{3,2,1,0:T(8,128)(2,1)S(1)}, bf16[3,2,512,128]{3,2,1,0:T(8,128)(2,1)S(1)}, u32[]{:S(2)}, u32[]{:S(2)}) %collective-permute-start.9) | collective-permute-done | bytes 786464 | tf_op jit(solution)/shard_map/partner_2/ppermute | solution.py:295
  56.6 1.9 %collective-permute-start.10 = (bf16[3,2,512,128]{3,2,1,0:T(8,128)(2,1)S(1)}, bf16[3,2,512,128]{3,2,1,0:T(8,128)(2,1)S(1)}, u32[]{:S(2)}, u32[]{:S(2)}) collective-permute-start(bf16[3,2,512,128]{3,2,1,0:T(8,128)(2,1)S(1)} %collective-permute-done.9.refs_1_), channel_id=1, source_target_pairs={{0,2},{2,4},{4,6},{6,8},{8,10},{10,12},{12,14},{14,16},{16,18},{18... | collective-permute-start | bytes 2359304 | tf_op jit(solution)/shard_map/onward_2/ppermute | solution.py:318
  58.5 1.6 %collective-permute-start = (bf16[1,2,384,128]{3,2,1,0:T(8,128)(2,1)S(1)}, bf16[1,2,384,128]{3,2,1,0:T(8,128)(2,1)S(1)}, u32[]{:S(2)}, u32[]{:S(2)}) collective-permute-start(bf16[1,2,384,128]{3,2,1,0:T(8,128)(2,1)S(1)} %get-tuple-element.25), channel_id=1, source_target_pairs={{0,1},{1,0},{2,3},{3,2},{4,5},{5,4},{6,7},{7,6},{8,9},{9,8},{10,11... | collective-permute-start | bytes 589832 | tf_op jit(solution)/shard_map/partner_4/ppermute | solution.py:295
  60.1 3.8 %attend_1.1.refs_6_ = f32[512,1536]{1,0:T(8,128)S(1)} custom-call(s32[8,5]{1,0:T(8,128)S(1)} %copy-done.3, s32[8]{0:T(128)S(1)} %copy-done.4, bf16[3,512,128]{2,1,0:T(8,128)(2,1)S(1)} %get-tuple-element.27.q_ref, bf16[3,2,512,128]{3,2,1,0:T(8,128)(2,1)S(1)} %get-tuple-element.28.refs_0_, bf16[3,2,512,128]{3,2,1,0:T(8,128)(2,1)S(1)} %collective-permute-done.2.refs_1_, ...), custom_call_target="tpu_custom_call" | custom-call | tf_op jit(solution)/shard_map/attend_1/pallas_call | solution.py:247
  63.9 1.0 %collective-permute-done.7.refs_1_ = bf16[2,2,384,128]{3,2,1,0:T(8,128)(2,1)S(1)} collective-permute-done((bf16[2,2,384,128]{3,2,1,0:T(8,128)(2,1)S(1)}, bf16[2,2,384,128]{3,2,1,0:T(8,128)(2,1)S(1)}, u32[]{:S(2)}, u32[]{:S(2)}) %collective-permute-start.7) | collective-permute-done | bytes 393248 | tf_op jit(solution)/shard_map/partner_3/ppermute | solution.py:295
  64.9 1.9 %collective-permute-start.8 = (bf16[2,2,384,128]{3,2,1,0:T(8,128)(2,1)S(1)}, bf16[2,2,384,128]{3,2,1,0:T(8,128)(2,1)S(1)}, u32[]{:S(2)}, u32[]{:S(2)}) collective-permute-start(bf16[2,2,384,128]{3,2,1,0:T(8,128)(2,1)S(1)} %collective-permute-done.7.refs_1_), channel_id=1, source_target_pairs={{0,2},{2,4},{4,6},{6,8},{8,10},{10,12},{12,14},{14,16},{16,18},{18... | collective-permute-start | bytes 1179656 | tf_op jit(solution)/shard_map/onward_3/ppermute | solution.py:318
  66.8 2.0 %collective-permute-start.1 = (bf16[3,2,128,128]{3,2,1,0:T(8,128)(2,1)S(1)}, bf16[3,2,128,128]{3,2,1,0:T(8,128)(2,1)S(1)}, u32[]{:S(2)}, u32[]{:S(2)}) collective-permute-start(bf16[3,2,128,128]{3,2,1,0:T(8,128)(2,1)S(1)} %get-tuple-element.26), channel_id=1, source_target_pairs={{0,1},{1,0},{2,3},{3,2},{4,5},{5,4},{6,7},{7,6},{8,9},{9,8},{10,11... | collective-permute-start | bytes 589832 | tf_op jit(solution)/shard_map/rest_5/ppermute | solution.py:295
  68.8 2.1 %collective-permute-start.6 = (bf16[1,2,384,128]{3,2,1,0:T(8,128)(2,1)S(1)}, bf16[1,2,384,128]{3,2,1,0:T(8,128)(2,1)S(1)}, u32[]{:S(2)}, u32[]{:S(2)}) collective-permute-start(bf16[1,2,384,128]{3,2,1,0:T(8,128)(2,1)S(1)} %collective-permute-done.refs_1_), channel_id=1, source_target_pairs={{0,2},{2,4},{4,6},{6,8},{8,10},{10,12},{12,14},{14,16},{16,18},{18... | collective-permute-start | bytes 589832 | tf_op jit(solution)/shard_map/onward_4/ppermute | solution.py:318
  70.9 2.6 %attend_2.1.refs_4_ = bf16[512,384]{1,0:T(8,128)(2,1)S(1)} custom-call(s32[8,5]{1,0:T(8,128)S(1)} %copy-done.3, s32[8]{0:T(128)S(1)} %copy-done.4, bf16[3,512,128]{2,1,0:T(8,128)(2,1)S(1)} %get-tuple-element.36.q_ref, bf16[3,2,512,128]{3,2,1,0:T(8,128)(2,1)S(1)} %get-tuple-element.37.refs_0_, bf16[3,2,512,128]{3,2,1,0:T(8,128)(2,1)S(1)} %collective-permute-done.9.refs_1_, ...), custom_call_target="tpu_custom_call" | custom-call | tf_op jit(solution)/shard_map/attend_2/pallas_call | solution.py:247
  75.0 2.0 %attend_3.1.refs_4_ = bf16[512,640]{1,0:T(8,128)(2,1)S(1)} custom-call(s32[8,5]{1,0:T(8,128)S(1)} %copy-done.3, s32[8]{0:T(128)S(1)} %copy-done.4, bf16[2,512,128]{2,1,0:T(8,128)(2,1)S(1)} %get-tuple-element.32.q_ref, bf16[2,2,512,128]{3,2,1,0:T(8,128)(2,1)S(1)} %get-tuple-element.33.refs_0_, bf16[2,2,384,128]{3,2,1,0:T(8,128)(2,1)S(1)} %collective-permute-done.7.refs_1_, ...), custom_call_target="tpu_custom_call" | custom-call | tf_op jit(solution)/shard_map/attend_3/pallas_call | solution.py:247
  77.1 3.5 %attend_4.1 = bf16[512,1536]{1,0:T(8,128)(2,1)} custom-call(s32[8,5]{1,0:T(8,128)S(1)} %copy-done.3, s32[8]{0:T(128)S(1)} %copy-done.4, bf16[1,512,128]{2,1,0:T(8,128)(2,1)S(1)} %get-tuple-element.23.q_ref, bf16[1,2,512,128]{3,2,1,0:T(8,128)(2,1)S(1)} %get-tuple-element.24.refs_0_, bf16[1,2,384,128]{3,2,1,0:T(8,128)(2,1)S(1)} %collective-permute-done.refs_1_, ...), custom_call_target="tpu_custom_call" | custom-call | tf_op jit(solution)/shard_map/attend_4/pallas_call | solution.py:247
  (20 shorter events, 2.5 us)
Async XLA Ops:
  0.0 60.0 %slice-start = ((s8[4718592]{0:T(1024)(128)(4,1)}), s8[524288]{0:T(1024)(128)(4,1)S(1)}, s32[]{:S(2)}) async-start(s8[4718592]{0:T(1024)(128)(4,1)} %bitcast), calls=%async_computation | async-start | bytes 1048576
  2.1 57.9 %slice-start.1 = ((s8[4718592]{0:T(1024)(128)(4,1)}), s8[4194304]{0:T(1024)(128)(4,1)S(1)}, s32[]{:S(2)}) async-start(s8[4718592]{0:T(1024)(128)(4,1)} %bitcast), calls=%async_computation.1 | async-start | bytes 8388608
  2.1 20.7 %collective-permute-start.4 = (bf16[3,2,512,128]{3,2,1,0:T(8,128)(2,1)}, bf16[3,2,512,128]{3,2,1,0:T(8,128)(2,1)S(1)}, u32[]{:S(2)}, u32[]{:S(2)}) collective-permute-start(bf16[3,2,512,128]{3,2,1,0:T(8,128)(2,1)} %shard_map.64), channel_id=1, source_target_pairs={{0,1},{1,0},{2,3},{3,2},{4,5},{5,4},{6,7},{7,6},{8,9},{9,8},{10,11... | collective-permute-start | bytes 2359304 | tf_op jit(solution)/shard_map/partner_0/ppermute | solution.py:295
  3.7 1.4 %copy-start = (bf16[512,1536]{1,0:T(8,128)(2,1)S(1)}, bf16[512,1536]{1,0:T(8,128)(2,1)}, u32[]{:S(2)}) copy-start(bf16[512,1536]{1,0:T(8,128)(2,1)} %refs_0_.3) | copy-start | bytes 4718596
  5.1 1.4 %copy-start.1 = (bf16[512,1536]{1,0:T(8,128)(2,1)S(1)}, bf16[512,1536]{1,0:T(8,128)(2,1)}, u32[]{:S(2)}) copy-start(bf16[512,1536]{1,0:T(8,128)(2,1)} %refs_1_.2) | copy-start | bytes 4718596
  6.5 1.4 %copy-start.2 = (bf16[512,1536]{1,0:T(8,128)(2,1)S(1)}, bf16[512,1536]{1,0:T(8,128)(2,1)}, u32[]{:S(2)}) copy-start(bf16[512,1536]{1,0:T(8,128)(2,1)} %refs_2_.3) | copy-start | bytes 4718596
  7.9 35.3 %copy-start.3 = (s32[8,5]{1,0:T(8,128)S(1)}, s32[8,5]{1,0:T(8,128)}, u32[]{:S(2)}) copy-start(s32[8,5]{1,0:T(8,128)} %tiles_ref.9) | copy-start | bytes 484
  7.9 35.3 %copy-start.4 = (s32[8]{0:T(128)S(1)}, s32[8]{0:T(128)}, u32[]{:S(2)}) copy-start(s32[8]{0:T(128)} %counts_ref.9) | copy-start | bytes 100
  13.3 26.4 %collective-permute-start.2 = (bf16[3,2,512,128]{3,2,1,0:T(8,128)(2,1)S(1)}, bf16[3,2,512,128]{3,2,1,0:T(8,128)(2,1)S(1)}, u32[]{:S(2)}, u32[]{:S(2)}) collective-permute-start(bf16[3,2,512,128]{3,2,1,0:T(8,128)(2,1)S(1)} %get-tuple-element.28.refs_0_), channel_id=1, source_target_pairs={{0,1},{1,0},{2,3},{3,2},{4,5},{5,4},{6,7},{7,6},{8,9},{9,8},{10,11... | collective-permute-start | bytes 2359304 | tf_op jit(solution)/shard_map/partner_1/ppermute | solution.py:295
  22.9 20.3 %collective-permute-start.5 = (bf16[3,2,512,128]{3,2,1,0:T(8,128)(2,1)S(1)}, bf16[3,2,512,128]{3,2,1,0:T(8,128)(2,1)S(1)}, u32[]{:S(2)}, u32[]{:S(2)}) collective-permute-start(bf16[3,2,512,128]{3,2,1,0:T(8,128)(2,1)S(1)} %collective-permute-done.4.refs_1_), channel_id=1, source_target_pairs={{0,2},{2,4},{4,6},{6,8},{8,10},{10,12},{12,14},{14,16},{16,18},{18... | collective-permute-start | bytes 2359304 | tf_op jit(solution)/shard_map/onward_0/ppermute | solution.py:318
  24.8 31.8 %collective-permute-start.9 = (bf16[3,2,512,128]{3,2,1,0:T(8,128)(2,1)S(1)}, bf16[3,2,512,128]{3,2,1,0:T(8,128)(2,1)S(1)}, u32[]{:S(2)}, u32[]{:S(2)}) collective-permute-start(bf16[3,2,512,128]{3,2,1,0:T(8,128)(2,1)S(1)} %get-tuple-element.37.refs_0_), channel_id=1, source_target_pairs={{0,1},{1,0},{2,3},{3,2},{4,5},{5,4},{6,7},{7,6},{8,9},{9,8},{10,11... | collective-permute-start | bytes 2359304 | tf_op jit(solution)/shard_map/partner_2/ppermute | solution.py:295
  39.7 20.3 %collective-permute-start.3 = (bf16[3,2,512,128]{3,2,1,0:T(8,128)(2,1)S(1)}, bf16[3,2,512,128]{3,2,1,0:T(8,128)(2,1)S(1)}, u32[]{:S(2)}, u32[]{:S(2)}) collective-permute-start(bf16[3,2,512,128]{3,2,1,0:T(8,128)(2,1)S(1)} %collective-permute-done.2.refs_1_), channel_id=1, source_target_pairs={{0,2},{2,4},{4,6},{6,8},{8,10},{10,12},{12,14},{14,16},{16,18},{18... | collective-permute-start | bytes 2359304 | tf_op jit(solution)/shard_map/onward_1/ppermute | solution.py:318
  41.6 23.2 %collective-permute-start.7 = (bf16[2,2,384,128]{3,2,1,0:T(8,128)(2,1)S(1)}, bf16[2,2,384,128]{3,2,1,0:T(8,128)(2,1)S(1)}, u32[]{:S(2)}, u32[]{:S(2)}) collective-permute-start(bf16[2,2,384,128]{3,2,1,0:T(8,128)(2,1)S(1)} %get-tuple-element.34), channel_id=1, source_target_pairs={{0,1},{1,0},{2,3},{3,2},{4,5},{5,4},{6,7},{7,6},{8,9},{9,8},{10,11... | collective-permute-start | bytes 1179656 | tf_op jit(solution)/shard_map/partner_3/ppermute | solution.py:295
  56.6 14.3 %collective-permute-start.10 = (bf16[3,2,512,128]{3,2,1,0:T(8,128)(2,1)S(1)}, bf16[3,2,512,128]{3,2,1,0:T(8,128)(2,1)S(1)}, u32[]{:S(2)}, u32[]{:S(2)}) collective-permute-start(bf16[3,2,512,128]{3,2,1,0:T(8,128)(2,1)S(1)} %collective-permute-done.9.refs_1_), channel_id=1, source_target_pairs={{0,2},{2,4},{4,6},{6,8},{8,10},{10,12},{12,14},{14,16},{16,18},{18... | collective-permute-start | bytes 2359304 | tf_op jit(solution)/shard_map/onward_2/ppermute | solution.py:318
  58.5 10.3 %collective-permute-start = (bf16[1,2,384,128]{3,2,1,0:T(8,128)(2,1)S(1)}, bf16[1,2,384,128]{3,2,1,0:T(8,128)(2,1)S(1)}, u32[]{:S(2)}, u32[]{:S(2)}) collective-permute-start(bf16[1,2,384,128]{3,2,1,0:T(8,128)(2,1)S(1)} %get-tuple-element.25), channel_id=1, source_target_pairs={{0,1},{1,0},{2,3},{3,2},{4,5},{5,4},{6,7},{7,6},{8,9},{9,8},{10,11... | collective-permute-start | bytes 589832 | tf_op jit(solution)/shard_map/partner_4/ppermute | solution.py:295
  64.9 10.1 %collective-permute-start.8 = (bf16[2,2,384,128]{3,2,1,0:T(8,128)(2,1)S(1)}, bf16[2,2,384,128]{3,2,1,0:T(8,128)(2,1)S(1)}, u32[]{:S(2)}, u32[]{:S(2)}) collective-permute-start(bf16[2,2,384,128]{3,2,1,0:T(8,128)(2,1)S(1)} %collective-permute-done.7.refs_1_), channel_id=1, source_target_pairs={{0,2},{2,4},{4,6},{6,8},{8,10},{10,12},{12,14},{14,16},{16,18},{18... | collective-permute-start | bytes 1179656 | tf_op jit(solution)/shard_map/onward_3/ppermute | solution.py:318
  66.8 7.2 %collective-permute-start.1 = (bf16[3,2,128,128]{3,2,1,0:T(8,128)(2,1)S(1)}, bf16[3,2,128,128]{3,2,1,0:T(8,128)(2,1)S(1)}, u32[]{:S(2)}, u32[]{:S(2)}) collective-permute-start(bf16[3,2,128,128]{3,2,1,0:T(8,128)(2,1)S(1)} %get-tuple-element.26), channel_id=1, source_target_pairs={{0,1},{1,0},{2,3},{3,2},{4,5},{5,4},{6,7},{7,6},{8,9},{9,8},{10,11... | collective-permute-start | bytes 589832 | tf_op jit(solution)/shard_map/rest_5/ppermute | solution.py:295
  68.8 8.3 %collective-permute-start.6 = (bf16[1,2,384,128]{3,2,1,0:T(8,128)(2,1)S(1)}, bf16[1,2,384,128]{3,2,1,0:T(8,128)(2,1)S(1)}, u32[]{:S(2)}, u32[]{:S(2)}) collective-permute-start(bf16[1,2,384,128]{3,2,1,0:T(8,128)(2,1)S(1)} %collective-permute-done.refs_1_), channel_id=1, source_target_pairs={{0,2},{2,4},{4,6},{6,8},{8,10},{10,12},{12,14},{14,16},{16,18},{18... | collective-permute-start | bytes 589832 | tf_op jit(solution)/shard_map/onward_4/ppermute | solution.py:318

commit v2 on v1

--- a/solution.py
+++ b/solution.py
@@ -191,7 +191,22 @@
                 kv_buf[h % 2, part, place] = ref[h + shifts[i], part]
         kv_buf[h % 2, 1, spans : spans + TILE] = zeros
 
+    strips = []
+    if final and lead:
+        strips = list(range(0, w_ref.shape[1], STRIP))
+
+    def lay_strip(at):
+        here = slice(at, min(at + STRIP, w_ref.shape[1]))
+        weights = w_ref[(low - lead) * HD : low * HD, here]
+        part = jnp.dot(att_buf[:, : lead * HD], weights, preferred_element_type=jnp.float32)
+        if has_acc:
+            part = part + acc_ref[:, here]
+        sum_buf[:, here] = part
+
+    if final:
+        sum_buf = refs[5]
     jobs = [(h, tile) for h in range(size) for tile in range(tiles)]
+    share = -(-len(strips) // len(jobs))
     ready(0)
     ahead = scores(*jobs[0])
     for i, (h, tile) in enumerate(jobs):
@@ -200,17 +215,22 @@
             if jobs[i + 1][0] != h:
                 ready(h + 1)
             ahead = scores(*jobs[i + 1])
+        for at in strips[i * share : (i + 1) * share]:
+            lay_strip(at)
         finish(h, tile, now)
 
     if not projects:
         return
     stores = []
-    out_buf, out_sems = refs[3:] if final else (out_ref, None)
+    out_buf, out_sems = refs[3:5] if final else (out_ref, None)
+    skip = lead if strips else 0
     for i, at in enumerate(range(0, out_buf.shape[1], STRIP)):
         here = slice(at, min(at + STRIP, out_buf.shape[1]))
-        weights = w_ref[(low - lead) * HD : (low + size) * HD, here]
-        part = jnp.dot(att_buf[...], weights, preferred_element_type=jnp.float32)
-        if has_acc:
+        weights = w_ref[(low - lead + skip) * HD : (low + size) * HD, here]
+        part = jnp.dot(att_buf[:, skip * HD :], weights, preferred_element_type=jnp.float32)
+        if strips:
+            part = part + sum_buf[:, here]
+        elif has_acc:
             part = part + acc_ref[:, here]
         out_buf[:, here] = part.astype(out_buf.dtype)
         if final:
@@ -244,6 +264,7 @@
         out_shape = jax.ShapeDtypeStruct((rows, width), bf16 if final else jnp.float32)
         if final:
             scratch += [pltpu.VMEM((rows, width), bf16), pltpu.SemaphoreType.DMA((-(-width // STRIP),))]
+            scratch.append(pltpu.VMEM((rows, width), jnp.float32))
     return pl.pallas_call(
         functools.partial(
             attend_kernel, (low, size, shifts, layout, parts, projects, acc is not None, final)
@@ -252,7 +273,7 @@
         in_specs=[SMEM] * 2 + [VMEM] * (len(operands) - 2),
         out_specs=HBM if final else VMEM,
         scratch_shapes=scratch,
-        compiler_params=pltpu.CompilerParams(vmem_limit_bytes=VMEM_LIMIT),
+        compiler_params=pltpu.CompilerParams(vmem_limit_bytes=VMEM_LIMIT * (2 if final else 1)),
         cost_estimate=pl.CostEstimate(flops=0, bytes_accessed=0, transcendentals=0),
     )(*operands)
 

time: 81.8 us -> 82.1 us (level)
  no operation moved by 1% of the time
where the time goes in v2:
time: 82.1 us; the launch traced here: 81.1 us
  waiting for transfers between devices  35.5 us (43%)
  Pallas kernels  22.2 us (27%)
  starting transfers between devices  18.8 us (23%)
  local copies, waits for them, and re-layouts  4.24 us (5%)
    ppermute x6, waiting for transfers between devices, on_device(): near.append([lax.ppermute(block, 'ulysses', [(0, 1), (1, 0)])])  34.5 us
    pallas_call x5, Pallas kernels, attend(): pl.pallas_call(functools.partial(attend_kernel, (low, size, shifts, layou...  14.8 us
    ppermute x5, starting transfers between devices, on_device(): pieces.append(lax.ppermute(gate, both, onward))  9.73 us
    ppermute x6, starting transfers between devices, on_device(): near.append([lax.ppermute(block, 'ulysses', [(0, 1), (1, 0)])])  9.1 us
    pallas_call x2, Pallas kernels, pack(): pl.pallas_call(functools.partial(pack_kernel, groups, q_groups, cuts), ou...  7.45 us
    unnamed x14, local copies, waits for them, and re-layouts  4.24 us
  transfers between devices with their start and end apart: 11, of which 7 were waited for; matrix products, arithmetic and copies ran while one was open for 0% of the time, Pallas kernels for 20%

profile of v2, /device:TPU:8, one launch (start us, length us, event | category | flops | bytes accessed | tf_op | source)
XLA Modules:
  0.0 81.1 jit_solution(2143037361486510127)
XLA Ops:
  0.0 2.1 %shard_map.64 = bf16[3,2,512,128]{3,2,1,0:T(8,128)(2,1)} custom-call(bf16[512,1536]{1,0:T(8,128)(2,1)} %refs_0_.3, bf16[512,1536]{1,0:T(8,128)(2,1)} %refs_1_.2, bf16[512,1536]{1,0:T(8,128)(2,1)} %refs_2_.3), custom_call_target="tpu_custom_call" | custom-call | bytes 1572864 | tf_op jit(solution)/shard_map/pallas_call | solution.py:117
  2.1 1.6 %collective-permute-start.4 = (bf16[3,2,512,128]{3,2,1,0:T(8,128)(2,1)}, bf16[3,2,512,128]{3,2,1,0:T(8,128)(2,1)S(1)}, u32[]{:S(2)}, u32[]{:S(2)}) collective-permute-start(bf16[3,2,512,128]{3,2,1,0:T(8,128)(2,1)} %shard_map.64), channel_id=1, source_target_pairs={{0,1},{1,0},{2,3},{3,2},{4,5},{5,4},{6,7},{7,6},{8,9},{9,8},{10,11... | collective-permute-start | bytes 2359304 | tf_op jit(solution)/shard_map/partner_0/ppermute | solution.py:316
  3.7 1.4 %copy-done = bf16[512,1536]{1,0:T(8,128)(2,1)S(1)} copy-done((bf16[512,1536]{1,0:T(8,128)(2,1)S(1)}, bf16[512,1536]{1,0:T(8,128)(2,1)}, u32[]{:S(2)}) %copy-start) | copy-done | bytes 1572888
  5.1 1.4 %copy-done.1 = bf16[512,1536]{1,0:T(8,128)(2,1)S(1)} copy-done((bf16[512,1536]{1,0:T(8,128)(2,1)S(1)}, bf16[512,1536]{1,0:T(8,128)(2,1)}, u32[]{:S(2)}) %copy-start.1) | copy-done | bytes 1572888
  6.5 1.4 %copy-done.2 = bf16[512,1536]{1,0:T(8,128)(2,1)S(1)} copy-done((bf16[512,1536]{1,0:T(8,128)(2,1)S(1)}, bf16[512,1536]{1,0:T(8,128)(2,1)}, u32[]{:S(2)}) %copy-start.2) | copy-done | bytes 1572888
  7.9 5.3 %shard_map.65 = (bf16[3,2,512,128]{3,2,1,0:T(8,128)(2,1)S(1)}, bf16[3,2,512,128]{3,2,1,0:T(8,128)(2,1)S(1)}, bf16[3,2,512,128]{3,2,1,0:T(8,128)(2,1)S(1)}, bf16[...) custom-call(bf16[512,1536]{1,0:T(8,128)(2,1)S(1)} %copy-done, ...), custom_call_target="tpu_custom_call" | custom-call | bytes 6291456 | tf_op jit(solution)/shard_map/pallas_call | solution.py:117
  14.2 8.7 %collective-permute-done.4.refs_1_ = bf16[3,2,512,128]{3,2,1,0:T(8,128)(2,1)S(1)} collective-permute-done((bf16[3,2,512,128]{3,2,1,0:T(8,128)(2,1)}, bf16[3,2,512,128]{3,2,1,0:T(8,128)(2,1)S(1)}, u32[]{:S(2)}, u32[]{:S(2)}) %collective-permute-start.4) | collective-permute-done | bytes 786464 | tf_op jit(solution)/shard_map/partner_0/ppermute | solution.py:316
  22.9 1.9 %collective-permute-start.5 = (bf16[3,2,512,128]{3,2,1,0:T(8,128)(2,1)S(1)}, bf16[3,2,512,128]{3,2,1,0:T(8,128)(2,1)S(1)}, u32[]{:S(2)}, u32[]{:S(2)}) collective-permute-start(bf16[3,2,512,128]{3,2,1,0:T(8,128)(2,1)S(1)} %collective-permute-done.4.refs_1_), channel_id=1, source_target_pairs={{0,2},{2,4},{4,6},{6,8},{8,10},{10,12},{12,14},{14,16},{16,18},{18... | collective-permute-start | bytes 2359304 | tf_op jit(solution)/shard_map/onward_0/ppermute | solution.py:339
  24.8 1.6 %collective-permute-start.9 = (bf16[3,2,512,128]{3,2,1,0:T(8,128)(2,1)S(1)}, bf16[3,2,512,128]{3,2,1,0:T(8,128)(2,1)S(1)}, u32[]{:S(2)}, u32[]{:S(2)}) collective-permute-start(bf16[3,2,512,128]{3,2,1,0:T(8,128)(2,1)S(1)} %get-tuple-element.37.refs_0_), channel_id=1, source_target_pairs={{0,1},{1,0},{2,3},{3,2},{4,5},{5,4},{6,7},{7,6},{8,9},{9,8},{10,11... | collective-permute-start | bytes 2359304 | tf_op jit(solution)/shard_map/partner_2/ppermute | solution.py:316
  26.3 13.4 %collective-permute-done.2.refs_1_ = bf16[3,2,512,128]{3,2,1,0:T(8,128)(2,1)S(1)} collective-permute-done((bf16[3,2,512,128]{3,2,1,0:T(8,128)(2,1)S(1)}, bf16[3,2,512,128]{3,2,1,0:T(8,128)(2,1)S(1)}, u32[]{:S(2)}, u32[]{:S(2)}) %collective-permute-start.2) | collective-permute-done | bytes 786464 | tf_op jit(solution)/shard_map/partner_1/ppermute | solution.py:316
  39.7 1.9 %collective-permute-start.3 = (bf16[3,2,512,128]{3,2,1,0:T(8,128)(2,1)S(1)}, bf16[3,2,512,128]{3,2,1,0:T(8,128)(2,1)S(1)}, u32[]{:S(2)}, u32[]{:S(2)}) collective-permute-start(bf16[3,2,512,128]{3,2,1,0:T(8,128)(2,1)S(1)} %collective-permute-done.2.refs_1_), channel_id=1, source_target_pairs={{0,2},{2,4},{4,6},{6,8},{8,10},{10,12},{12,14},{14,16},{16,18},{18... | collective-permute-start | bytes 2359304 | tf_op jit(solution)/shard_map/onward_1/ppermute | solution.py:339
  41.6 1.6 %collective-permute-start.7 = (bf16[2,2,384,128]{3,2,1,0:T(8,128)(2,1)S(1)}, bf16[2,2,384,128]{3,2,1,0:T(8,128)(2,1)S(1)}, u32[]{:S(2)}, u32[]{:S(2)}) collective-permute-start(bf16[2,2,384,128]{3,2,1,0:T(8,128)(2,1)S(1)} %get-tuple-element.34), channel_id=1, source_target_pairs={{0,1},{1,0},{2,3},{3,2},{4,5},{5,4},{6,7},{7,6},{8,9},{9,8},{10,11... | collective-permute-start | bytes 1179656 | tf_op jit(solution)/shard_map/partner_3/ppermute | solution.py:316
  43.2 2.5 %attend_0.1.refs_3_ = bf16[512,384]{1,0:T(8,128)(2,1)S(1)} custom-call(s32[8,5]{1,0:T(8,128)S(1)} %copy-done.3, s32[8]{0:T(128)S(1)} %copy-done.4, bf16[3,512,128]{2,1,0:T(8,128)(2,1)S(1)} %get-tuple-element.29.q_ref, bf16[3,2,512,128]{3,2,1,0:T(8,128)(2,1)S(1)} %get-tuple-element.30.refs_0_, bf16[3,2,512,128]{3,2,1,0:T(8,128)(2,1)S(1)} %collective-permute-done.4.refs_1_, ...), custom_call_target="tpu_custom_call" | custom-call | tf_op jit(solution)/shard_map/attend_0/pallas_call | solution.py:268
  45.7 10.8 %collective-permute-done.9.refs_1_ = bf16[3,2,512,128]{3,2,1,0:T(8,128)(2,1)S(1)} collective-permute-done((bf16[3,2,512,128]{3,2,1,0:T(8,128)(2,1)S(1)}, bf16[3,2,512,128]{3,2,1,0:T(8,128)(2,1)S(1)}, u32[]{:S(2)}, u32[]{:S(2)}) %collective-permute-start.9) | collective-permute-done | bytes 786464 | tf_op jit(solution)/shard_map/partner_2/ppermute | solution.py:316
  56.6 1.9 %collective-permute-start.10 = (bf16[3,2,512,128]{3,2,1,0:T(8,128)(2,1)S(1)}, bf16[3,2,512,128]{3,2,1,0:T(8,128)(2,1)S(1)}, u32[]{:S(2)}, u32[]{:S(2)}) collective-permute-start(bf16[3,2,512,128]{3,2,1,0:T(8,128)(2,1)S(1)} %collective-permute-done.9.refs_1_), channel_id=1, source_target_pairs={{0,2},{2,4},{4,6},{6,8},{8,10},{10,12},{12,14},{14,16},{16,18},{18... | collective-permute-start | bytes 2359304 | tf_op jit(solution)/shard_map/onward_2/ppermute | solution.py:339
  58.5 1.6 %collective-permute-start = (bf16[1,2,384,128]{3,2,1,0:T(8,128)(2,1)S(1)}, bf16[1,2,384,128]{3,2,1,0:T(8,128)(2,1)S(1)}, u32[]{:S(2)}, u32[]{:S(2)}) collective-permute-start(bf16[1,2,384,128]{3,2,1,0:T(8,128)(2,1)S(1)} %get-tuple-element.25), channel_id=1, source_target_pairs={{0,1},{1,0},{2,3},{3,2},{4,5},{5,4},{6,7},{7,6},{8,9},{9,8},{10,11... | collective-permute-start | bytes 589832 | tf_op jit(solution)/shard_map/partner_4/ppermute | solution.py:316
  60.1 3.8 %attend_1.1.refs_6_ = f32[512,1536]{1,0:T(8,128)S(1)} custom-call(s32[8,5]{1,0:T(8,128)S(1)} %copy-done.3, s32[8]{0:T(128)S(1)} %copy-done.4, bf16[3,512,128]{2,1,0:T(8,128)(2,1)S(1)} %get-tuple-element.27.q_ref, bf16[3,2,512,128]{3,2,1,0:T(8,128)(2,1)S(1)} %get-tuple-element.28.refs_0_, bf16[3,2,512,128]{3,2,1,0:T(8,128)(2,1)S(1)} %collective-permute-done.2.refs_1_, ...), custom_call_target="tpu_custom_call" | custom-call | tf_op jit(solution)/shard_map/attend_1/pallas_call | solution.py:268
  63.9 1.0 %collective-permute-done.7.refs_1_ = bf16[2,2,384,128]{3,2,1,0:T(8,128)(2,1)S(1)} collective-permute-done((bf16[2,2,384,128]{3,2,1,0:T(8,128)(2,1)S(1)}, bf16[2,2,384,128]{3,2,1,0:T(8,128)(2,1)S(1)}, u32[]{:S(2)}, u32[]{:S(2)}) %collective-permute-start.7) | collective-permute-done | bytes 393248 | tf_op jit(solution)/shard_map/partner_3/ppermute | solution.py:316
  64.9 1.9 %collective-permute-start.8 = (bf16[2,2,384,128]{3,2,1,0:T(8,128)(2,1)S(1)}, bf16[2,2,384,128]{3,2,1,0:T(8,128)(2,1)S(1)}, u32[]{:S(2)}, u32[]{:S(2)}) collective-permute-start(bf16[2,2,384,128]{3,2,1,0:T(8,128)(2,1)S(1)} %collective-permute-done.7.refs_1_), channel_id=1, source_target_pairs={{0,2},{2,4},{4,6},{6,8},{8,10},{10,12},{12,14},{14,16},{16,18},{18... | collective-permute-start | bytes 1179656 | tf_op jit(solution)/shard_map/onward_3/ppermute | solution.py:339
  66.8 2.0 %collective-permute-start.1 = (bf16[3,2,128,128]{3,2,1,0:T(8,128)(2,1)S(1)}, bf16[3,2,128,128]{3,2,1,0:T(8,128)(2,1)S(1)}, u32[]{:S(2)}, u32[]{:S(2)}) collective-permute-start(bf16[3,2,128,128]{3,2,1,0:T(8,128)(2,1)S(1)} %get-tuple-element.26), channel_id=1, source_target_pairs={{0,1},{1,0},{2,3},{3,2},{4,5},{5,4},{6,7},{7,6},{8,9},{9,8},{10,11... | collective-permute-start | bytes 589832 | tf_op jit(solution)/shard_map/rest_5/ppermute | solution.py:316
  68.8 2.1 %collective-permute-start.6 = (bf16[1,2,384,128]{3,2,1,0:T(8,128)(2,1)S(1)}, bf16[1,2,384,128]{3,2,1,0:T(8,128)(2,1)S(1)}, u32[]{:S(2)}, u32[]{:S(2)}) collective-permute-start(bf16[1,2,384,128]{3,2,1,0:T(8,128)(2,1)S(1)} %collective-permute-done.refs_1_), channel_id=1, source_target_pairs={{0,2},{2,4},{4,6},{6,8},{8,10},{10,12},{12,14},{14,16},{16,18},{18... | collective-permute-start | bytes 589832 | tf_op jit(solution)/shard_map/onward_4/ppermute | solution.py:339
  70.9 2.5 %attend_2.1.refs_4_ = bf16[512,384]{1,0:T(8,128)(2,1)S(1)} custom-call(s32[8,5]{1,0:T(8,128)S(1)} %copy-done.3, s32[8]{0:T(128)S(1)} %copy-done.4, bf16[3,512,128]{2,1,0:T(8,128)(2,1)S(1)} %get-tuple-element.36.q_ref, bf16[3,2,512,128]{3,2,1,0:T(8,128)(2,1)S(1)} %get-tuple-element.37.refs_0_, bf16[3,2,512,128]{3,2,1,0:T(8,128)(2,1)S(1)} %collective-permute-done.9.refs_1_, ...), custom_call_target="tpu_custom_call" | custom-call | tf_op jit(solution)/shard_map/attend_2/pallas_call | solution.py:268
  75.0 2.0 %attend_3.1.refs_4_ = bf16[512,640]{1,0:T(8,128)(2,1)S(1)} custom-call(s32[8,5]{1,0:T(8,128)S(1)} %copy-done.3, s32[8]{0:T(128)S(1)} %copy-done.4, bf16[2,512,128]{2,1,0:T(8,128)(2,1)S(1)} %get-tuple-element.32.q_ref, bf16[2,2,512,128]{3,2,1,0:T(8,128)(2,1)S(1)} %get-tuple-element.33.refs_0_, bf16[2,2,384,128]{3,2,1,0:T(8,128)(2,1)S(1)} %collective-permute-done.7.refs_1_, ...), custom_call_target="tpu_custom_call" | custom-call | tf_op jit(solution)/shard_map/attend_3/pallas_call | solution.py:268
  77.1 3.9 %attend_4.1 = bf16[512,1536]{1,0:T(8,128)(2,1)} custom-call(s32[8,5]{1,0:T(8,128)S(1)} %copy-done.3, s32[8]{0:T(128)S(1)} %copy-done.4, bf16[1,512,128]{2,1,0:T(8,128)(2,1)S(1)} %get-tuple-element.23.q_ref, bf16[1,2,512,128]{3,2,1,0:T(8,128)(2,1)S(1)} %get-tuple-element.24.refs_0_, bf16[1,2,384,128]{3,2,1,0:T(8,128)(2,1)S(1)} %collective-permute-done.refs_1_, ...), custom_call_target="tpu_custom_call" | custom-call | tf_op jit(solution)/shard_map/attend_4/pallas_call | solution.py:268
  (20 shorter events, 2.6 us)
Async XLA Ops:
  0.0 60.0 %slice-start = ((s8[4718592]{0:T(1024)(128)(4,1)}), s8[524288]{0:T(1024)(128)(4,1)S(1)}, s32[]{:S(2)}) async-start(s8[4718592]{0:T(1024)(128)(4,1)} %bitcast), calls=%async_computation | async-start | bytes 1048576
  2.1 57.9 %slice-start.1 = ((s8[4718592]{0:T(1024)(128)(4,1)}), s8[4194304]{0:T(1024)(128)(4,1)S(1)}, s32[]{:S(2)}) async-start(s8[4718592]{0:T(1024)(128)(4,1)} %bitcast), calls=%async_computation.1 | async-start | bytes 8388608
  2.1 20.7 %collective-permute-start.4 = (bf16[3,2,512,128]{3,2,1,0:T(8,128)(2,1)}, bf16[3,2,512,128]{3,2,1,0:T(8,128)(2,1)S(1)}, u32[]{:S(2)}, u32[]{:S(2)}) collective-permute-start(bf16[3,2,512,128]{3,2,1,0:T(8,128)(2,1)} %shard_map.64), channel_id=1, source_target_pairs={{0,1},{1,0},{2,3},{3,2},{4,5},{5,4},{6,7},{7,6},{8,9},{9,8},{10,11... | collective-permute-start | bytes 2359304 | tf_op jit(solution)/shard_map/partner_0/ppermute | solution.py:316
  3.7 1.4 %copy-start = (bf16[512,1536]{1,0:T(8,128)(2,1)S(1)}, bf16[512,1536]{1,0:T(8,128)(2,1)}, u32[]{:S(2)}) copy-start(bf16[512,1536]{1,0:T(8,128)(2,1)} %refs_0_.3) | copy-start | bytes 4718596
  5.1 1.4 %copy-start.1 = (bf16[512,1536]{1,0:T(8,128)(2,1)S(1)}, bf16[512,1536]{1,0:T(8,128)(2,1)}, u32[]{:S(2)}) copy-start(bf16[512,1536]{1,0:T(8,128)(2,1)} %refs_1_.2) | copy-start | bytes 4718596
  6.5 1.4 %copy-start.2 = (bf16[512,1536]{1,0:T(8,128)(2,1)S(1)}, bf16[512,1536]{1,0:T(8,128)(2,1)}, u32[]{:S(2)}) copy-start(bf16[512,1536]{1,0:T(8,128)(2,1)} %refs_2_.3) | copy-start | bytes 4718596
  7.9 35.3 %copy-start.3 = (s32[8,5]{1,0:T(8,128)S(1)}, s32[8,5]{1,0:T(8,128)}, u32[]{:S(2)}) copy-start(s32[8,5]{1,0:T(8,128)} %tiles_ref.9) | copy-start | bytes 484
  7.9 35.3 %copy-start.4 = (s32[8]{0:T(128)S(1)}, s32[8]{0:T(128)}, u32[]{:S(2)}) copy-start(s32[8]{0:T(128)} %counts_ref.9) | copy-start | bytes 100
  13.3 26.4 %collective-permute-start.2 = (bf16[3,2,512,128]{3,2,1,0:T(8,128)(2,1)S(1)}, bf16[3,2,512,128]{3,2,1,0:T(8,128)(2,1)S(1)}, u32[]{:S(2)}, u32[]{:S(2)}) collective-permute-start(bf16[3,2,512,128]{3,2,1,0:T(8,128)(2,1)S(1)} %get-tuple-element.28.refs_0_), channel_id=1, source_target_pairs={{0,1},{1,0},{2,3},{3,2},{4,5},{5,4},{6,7},{7,6},{8,9},{9,8},{10,11... | collective-permute-start | bytes 2359304 | tf_op jit(solution)/shard_map/partner_1/ppermute | solution.py:316
  22.9 20.3 %collective-permute-start.5 = (bf16[3,2,512,128]{3,2,1,0:T(8,128)(2,1)S(1)}, bf16[3,2,512,128]{3,2,1,0:T(8,128)(2,1)S(1)}, u32[]{:S(2)}, u32[]{:S(2)}) collective-permute-start(bf16[3,2,512,128]{3,2,1,0:T(8,128)(2,1)S(1)} %collective-permute-done.4.refs_1_), channel_id=1, source_target_pairs={{0,2},{2,4},{4,6},{6,8},{8,10},{10,12},{12,14},{14,16},{16,18},{18... | collective-permute-start | bytes 2359304 | tf_op jit(solution)/shard_map/onward_0/ppermute | solution.py:339
  24.8 31.8 %collective-permute-start.9 = (bf16[3,2,512,128]{3,2,1,0:T(8,128)(2,1)S(1)}, bf16[3,2,512,128]{3,2,1,0:T(8,128)(2,1)S(1)}, u32[]{:S(2)}, u32[]{:S(2)}) collective-permute-start(bf16[3,2,512,128]{3,2,1,0:T(8,128)(2,1)S(1)} %get-tuple-element.37.refs_0_), channel_id=1, source_target_pairs={{0,1},{1,0},{2,3},{3,2},{4,5},{5,4},{6,7},{7,6},{8,9},{9,8},{10,11... | collective-permute-start | bytes 2359304 | tf_op jit(solution)/shard_map/partner_2/ppermute | solution.py:316
  39.7 20.3 %collective-permute-start.3 = (bf16[3,2,512,128]{3,2,1,0:T(8,128)(2,1)S(1)}, bf16[3,2,512,128]{3,2,1,0:T(8,128)(2,1)S(1)}, u32[]{:S(2)}, u32[]{:S(2)}) collective-permute-start(bf16[3,2,512,128]{3,2,1,0:T(8,128)(2,1)S(1)} %collective-permute-done.2.refs_1_), channel_id=1, source_target_pairs={{0,2},{2,4},{4,6},{6,8},{8,10},{10,12},{12,14},{14,16},{16,18},{18... | collective-permute-start | bytes 2359304 | tf_op jit(solution)/shard_map/onward_1/ppermute | solution.py:339
  41.6 23.2 %collective-permute-start.7 = (bf16[2,2,384,128]{3,2,1,0:T(8,128)(2,1)S(1)}, bf16[2,2,384,128]{3,2,1,0:T(8,128)(2,1)S(1)}, u32[]{:S(2)}, u32[]{:S(2)}) collective-permute-start(bf16[2,2,384,128]{3,2,1,0:T(8,128)(2,1)S(1)} %get-tuple-element.34), channel_id=1, source_target_pairs={{0,1},{1,0},{2,3},{3,2},{4,5},{5,4},{6,7},{7,6},{8,9},{9,8},{10,11... | collective-permute-start | bytes 1179656 | tf_op jit(solution)/shard_map/partner_3/ppermute | solution.py:316
  56.6 14.3 %collective-permute-start.10 = (bf16[3,2,512,128]{3,2,1,0:T(8,128)(2,1)S(1)}, bf16[3,2,512,128]{3,2,1,0:T(8,128)(2,1)S(1)}, u32[]{:S(2)}, u32[]{:S(2)}) collective-permute-start(bf16[3,2,512,128]{3,2,1,0:T(8,128)(2,1)S(1)} %collective-permute-done.9.refs_1_), channel_id=1, source_target_pairs={{0,2},{2,4},{4,6},{6,8},{8,10},{10,12},{12,14},{14,16},{16,18},{18... | collective-permute-start | bytes 2359304 | tf_op jit(solution)/shard_map/onward_2/ppermute | solution.py:339
  58.5 10.3 %collective-permute-start = (bf16[1,2,384,128]{3,2,1,0:T(8,128)(2,1)S(1)}, bf16[1,2,384,128]{3,2,1,0:T(8,128)(2,1)S(1)}, u32[]{:S(2)}, u32[]{:S(2)}) collective-permute-start(bf16[1,2,384,128]{3,2,1,0:T(8,128)(2,1)S(1)} %get-tuple-element.25), channel_id=1, source_target_pairs={{0,1},{1,0},{2,3},{3,2},{4,5},{5,4},{6,7},{7,6},{8,9},{9,8},{10,11... | collective-permute-start | bytes 589832 | tf_op jit(solution)/shard_map/partner_4/ppermute | solution.py:316
  64.9 10.1 %collective-permute-start.8 = (bf16[2,2,384,128]{3,2,1,0:T(8,128)(2,1)S(1)}, bf16[2,2,384,128]{3,2,1,0:T(8,128)(2,1)S(1)}, u32[]{:S(2)}, u32[]{:S(2)}) collective-permute-start(bf16[2,2,384,128]{3,2,1,0:T(8,128)(2,1)S(1)} %collective-permute-done.7.refs_1_), channel_id=1, source_target_pairs={{0,2},{2,4},{4,6},{6,8},{8,10},{10,12},{12,14},{14,16},{16,18},{18... | collective-permute-start | bytes 1179656 | tf_op jit(solution)/shard_map/onward_3/ppermute | solution.py:339
  66.8 7.2 %collective-permute-start.1 = (bf16[3,2,128,128]{3,2,1,0:T(8,128)(2,1)S(1)}, bf16[3,2,128,128]{3,2,1,0:T(8,128)(2,1)S(1)}, u32[]{:S(2)}, u32[]{:S(2)}) collective-permute-start(bf16[3,2,128,128]{3,2,1,0:T(8,128)(2,1)S(1)} %get-tuple-element.26), channel_id=1, source_target_pairs={{0,1},{1,0},{2,3},{3,2},{4,5},{5,4},{6,7},{7,6},{8,9},{9,8},{10,11... | collective-permute-start | bytes 589832 | tf_op jit(solution)/shard_map/rest_5/ppermute | solution.py:316
  68.8 8.3 %collective-permute-start.6 = (bf16[1,2,384,128]{3,2,1,0:T(8,128)(2,1)S(1)}, bf16[1,2,384,128]{3,2,1,0:T(8,128)(2,1)S(1)}, u32[]{:S(2)}, u32[]{:S(2)}) collective-permute-start(bf16[1,2,384,128]{3,2,1,0:T(8,128)(2,1)S(1)} %collective-permute-done.refs_1_), channel_id=1, source_target_pairs={{0,2},{2,4},{4,6},{6,8},{8,10},{10,12},{12,14},{14,16},{16,18},{18... | collective-permute-start | bytes 589832 | tf_op jit(solution)/shard_map/onward_4/ppermute | solution.py:339
